TPU v7x, 512 devices: a whole 4x4x16 slice. The times are simulated.
512 devices in a mesh: clus: 8 (over y, core), blk: 64 (over z, x).
Axes of the slice: x: 4, y: 4, z: 16, core: 2. Of those that a mesh axis runs over, the one named last changes fastest.
Arguments:
- embeddings: bfloat16 [262144, 1024], P(('clus', 'blk')), may hold values from -120 to 120
- cluster_sizes: int32 [170], replicated, may hold values from 1 to 5, 512 in all
Outputs:
- best_score: float32 [262144], P(('clus', 'blk'))
- soft_count: float32 [262144], P(('clus', 'blk'))
All inputs are finite; a program needn't handle non-finite values.
Results may differ from a plain program's by a relative error of at most 0.001.
Values may be sent and summed in bfloat16 or wider, within the bound.
No kernel may reach another device: no remote copies, remote signals or barrier semaphores. Data moves between devices by JAX's collectives and lax.ppermute only.
A program may use at most 64 MiB of HBM per device.

v0:
```python
import math

import jax
import jax.numpy as jnp
from jax import lax
from jax.sharding import PartitionSpec as P

MOST = 5


epsilon = 1e-06
threshold = 0.5
sharpness = 20.0
floor_value = -2.0


def passed_along(block, axis, distance):
    devices = range(lax.axis_size(axis))
    route = [(i - distance, i) for i in devices if i - distance in devices]
    return lax.ppermute(block, axis, route)


def unitize(values):
    widened = values.astype(jnp.float32)
    factor = lax.rsqrt(jnp.mean(widened * widened, axis=-1, keepdims=True) + epsilon) * (
        1.0 / math.sqrt(values.shape[-1])
    )
    return (widened * factor).astype(jnp.bfloat16)


def block_stats(mine_rows, other_rows):
    scores = lax.dot_general(
        mine_rows, other_rows, (((1,), (1,)), ((), ())), preferred_element_type=jnp.float32
    )
    closeness = jax.nn.sigmoid(sharpness * (scores - threshold))
    return (
        jnp.max(scores, axis=1),
        jnp.sum(closeness, axis=1),
        jnp.max(scores, axis=0),
        jnp.sum(closeness, axis=0),
    )


def empty_stats(length):
    lowest = jnp.full((length,), floor_value, jnp.float32)
    nought = jnp.zeros((length,), jnp.float32)
    return (lowest, nought, lowest, nought)


def diag_stats(mine_rows):
    scores = lax.dot_general(
        mine_rows, mine_rows, (((1,), (1,)), ((), ())), preferred_element_type=jnp.float32
    )
    length = mine_rows.shape[0]
    self_pair = lax.broadcasted_iota(jnp.int32, (length, length), 0) == lax.broadcasted_iota(
        jnp.int32, (length, length), 1
    )
    closeness = jnp.where(
        self_pair, jnp.float32(0.0), jax.nn.sigmoid(sharpness * (scores - threshold))
    )
    masked = jnp.where(self_pair, jnp.float32(floor_value), scores)
    return (jnp.max(masked, axis=1), jnp.sum(closeness, axis=1))


def pair_stats(mine_rows, other_rows, usable):
    length = mine_rows.shape[0]
    computed = block_stats(mine_rows, other_rows)
    fallback = empty_stats(length)
    return tuple((jnp.where(usable, value, spare) for value, spare in zip(computed, fallback)))


def shards(embeddings, cluster_sizes):
    normed = unitize(embeddings)
    position = lax.axis_index(("clus", "blk"))
    cluster_end = jnp.cumsum(cluster_sizes)
    cluster_start = cluster_end - cluster_sizes
    member = (cluster_start <= position) & (position < cluster_end)
    behind = position - jnp.sum(jnp.where(member, cluster_start, 0))
    forward = jnp.sum(jnp.where(member, cluster_end, 0)) - 1 - position
    best_score, soft_count = diag_stats(normed)
    for distance in range(1, MOST):
        before = passed_along(normed, ("clus", "blk"), distance)
        later_block = passed_along(normed, ("clus", "blk"), -distance)
        early_best, early_count, unused_best, unused_count = pair_stats(
            normed, before, distance <= behind
        )
        late_best, late_count, spare_best, spare_count = pair_stats(
            normed, later_block, distance <= forward
        )
        best_score = jnp.maximum(best_score, jnp.maximum(early_best, late_best))
        soft_count = soft_count + early_count + late_count
    return (best_score, soft_count)


def solution(mesh):
    return jax.shard_map(
        shards,
        mesh=mesh,
        in_specs=(P(("clus", "blk"), None), P()),
        out_specs=(P(("clus", "blk")), P(("clus", "blk"))),
        check_vma=False,
    )
```

profile of v0, /device:TPU:506, one launch (start us, length us, event | category | flops | bytes accessed | tf_op | source)
XLA Modules:
  0.0 121.9 jit_solution(16790900571536337412)
XLA Ops:
  0.6 0.0 copy-start
  0.6 1.6 %fusion = f32[512]{0:T(512)S(1)} fusion(bf16[512,1024]{1,0:T(8,128)(2,1)} %param.2), kind=kLoop, calls=%fused_computation.2 | loop fusion | flops 1572352 | bytes 1050624 | tf_op jit(solution)/shard_map/reduce_sum | solution.py:25
  2.2 0.0 copy-done
  2.2 0.0 copy-start.1
  2.3 0.2 fusion.1
  2.5 4.5 %collective-permute-start.3 = (bf16[512,1024]{1,0:T(8,128)(2,1)S(1)}, bf16[512,1024]{1,0:T(8,128)(2,1)}, u32[]{:S(2)}, u32[]{:S(2)}) collective-permute-start(bf16[512,1024]{1,0:T(8,128)(2,1)S(1)} %fusion.1), channel_id=1, source_target_pairs={{2,0},{3,1},{4,2},{5,3},{6,4},{7,5},{8,6},{9,7},{10,8},{11,9},{12,... | collective-permute-start | bytes 3145736 | tf_op jit(solution)/shard_map/ppermute | solution.py:20
  7.0 4.7 %collective-permute-start.4 = (bf16[512,1024]{1,0:T(8,128)(2,1)S(1)}, bf16[512,1024]{1,0:T(8,128)(2,1)}, u32[]{:S(2)}, u32[]{:S(2)}) collective-permute-start(bf16[512,1024]{1,0:T(8,128)(2,1)S(1)} %fusion.1), channel_id=1, source_target_pairs={{0,3},{1,4},{2,5},{3,6},{4,7},{5,8},{6,9},{7,10},{8,11},{9,12},{10... | collective-permute-start | bytes 3145736 | tf_op jit(solution)/shard_map/ppermute | solution.py:20
  11.7 2.0 %collective-permute-start.5 = (bf16[512,1024]{1,0:T(8,128)(2,1)S(1)}, bf16[512,1024]{1,0:T(8,128)(2,1)}, u32[]{:S(2)}, u32[]{:S(2)}) collective-permute-start(bf16[512,1024]{1,0:T(8,128)(2,1)S(1)} %fusion.1), channel_id=1, source_target_pairs={{3,0},{4,1},{5,2},{6,3},{7,4},{8,5},{9,6},{10,7},{11,8},{12,9},{13... | collective-permute-start | bytes 3145736 | tf_op jit(solution)/shard_map/ppermute | solution.py:20
  13.8 4.8 %collective-permute-start.6 = (bf16[512,1024]{1,0:T(8,128)(2,1)S(1)}, bf16[512,1024]{1,0:T(8,128)(2,1)S(1)}, u32[]{:S(2)}, u32[]{:S(2)}) collective-permute-start(bf16[512,1024]{1,0:T(8,128)(2,1)S(1)} %fusion.1), channel_id=1, source_target_pairs={{0,4},{1,5},{2,6},{3,7},{4,8},{5,9},{6,10},{7,11},{8,12},{9,13},{1... | collective-permute-start | bytes 3145736 | tf_op jit(solution)/shard_map/ppermute | solution.py:20
  18.5 1.9 %collective-permute-start = (bf16[512,1024]{1,0:T(8,128)(2,1)S(1)}, bf16[512,1024]{1,0:T(8,128)(2,1)S(1)}, u32[]{:S(2)}, u32[]{:S(2)}) collective-permute-start(bf16[512,1024]{1,0:T(8,128)(2,1)S(1)} %fusion.1), channel_id=1, source_target_pairs={{0,1},{1,2},{2,3},{3,4},{4,5},{5,6},{6,7},{7,8},{8,9},{9,10},{10,1... | collective-permute-start | bytes 3145736 | tf_op jit(solution)/shard_map/ppermute | solution.py:20
  20.5 0.0 copy-done.1
  20.5 0.3 reduce-window.9
  20.8 0.1 slice.10
  20.9 0.1 slice_reduce_fusion
  21.0 0.1 add_bitcast_fusion
  21.1 0.6 select_reduce_fusion.3
  23.1 0.9 select_reduce_fusion
  24.0 30.0 %collective-permute-done.3 = bf16[512,1024]{1,0:T(8,128)(2,1)} collective-permute-done((bf16[512,1024]{1,0:T(8,128)(2,1)S(1)}, bf16[512,1024]{1,0:T(8,128)(2,1)}, u32[]{:S(2)}, u32[]{:S(2)}) %collective-permute-start.3) | collective-permute-done | bytes 1048608 | tf_op jit(solution)/shard_map/ppermute | solution.py:20
  54.0 3.0 %collective-permute-start.1 = (bf16[512,1024]{1,0:T(8,128)(2,1)S(1)}, bf16[512,1024]{1,0:T(8,128)(2,1)S(1)}, u32[]{:S(2)}, u32[]{:S(2)}) collective-permute-start(bf16[512,1024]{1,0:T(8,128)(2,1)S(1)} %fusion.1), channel_id=1, source_target_pairs={{1,0},{2,1},{3,2},{4,3},{5,4},{6,5},{7,6},{8,7},{9,8},{10,9},{11,1... | collective-permute-start | bytes 3145736 | tf_op jit(solution)/shard_map/ppermute | solution.py:20
  57.0 2.1 %fusion.5 = (f32[512]{0:T(512)S(1)}, f32[512]{0:T(512)S(1)}) fusion(bf16[512,1024]{1,0:T(8,128)(2,1)S(1)} %fusion.1, bf16[512,1024]{1,0:T(8,128)(2,1)} %collective-permute-done.3), kind=kOutput, calls=%fused_computation.18 | convolution fusion | flops 538704896 | bytes 2101248 | tf_op jit(solution)/shard_map/dot_general | solution.py:32
  59.1 0.0 collective-permute-done.4
  59.1 1.9 %collective-permute-start.2 = (bf16[512,1024]{1,0:T(8,128)(2,1)S(1)}, bf16[512,1024]{1,0:T(8,128)(2,1)S(1)}, u32[]{:S(2)}, u32[]{:S(2)}) collective-permute-start(bf16[512,1024]{1,0:T(8,128)(2,1)S(1)} %fusion.1), channel_id=1, source_target_pairs={{0,2},{1,3},{2,4},{3,5},{4,6},{5,7},{6,8},{7,9},{8,10},{9,11},{10,... | collective-permute-start | bytes 3145736 | tf_op jit(solution)/shard_map/ppermute | solution.py:20
  61.1 2.1 %fusion.6 = (f32[512]{0:T(512)S(1)}, f32[512]{0:T(512)S(1)}) fusion(bf16[512,1024]{1,0:T(8,128)(2,1)S(1)} %fusion.1, bf16[512,1024]{1,0:T(8,128)(2,1)} %collective-permute-done.4), kind=kOutput, calls=%fused_computation.19 | convolution fusion | flops 538704896 | bytes 2101248 | tf_op jit(solution)/shard_map/dot_general | solution.py:32
  63.2 5.5 %collective-permute-done.5 = bf16[512,1024]{1,0:T(8,128)(2,1)} collective-permute-done((bf16[512,1024]{1,0:T(8,128)(2,1)S(1)}, bf16[512,1024]{1,0:T(8,128)(2,1)}, u32[]{:S(2)}, u32[]{:S(2)}) %collective-permute-start.5) | collective-permute-done | bytes 1048608 | tf_op jit(solution)/shard_map/ppermute | solution.py:20
  68.7 2.9 %collective-permute-start.7 = (bf16[512,1024]{1,0:T(8,128)(2,1)S(1)}, bf16[512,1024]{1,0:T(8,128)(2,1)S(1)}, u32[]{:S(2)}, u32[]{:S(2)}) collective-permute-start(bf16[512,1024]{1,0:T(8,128)(2,1)S(1)} %fusion.1), channel_id=1, source_target_pairs={{4,0},{5,1},{6,2},{7,3},{8,4},{9,5},{10,6},{11,7},{12,8},{13,9},{1... | collective-permute-start | bytes 3145736 | tf_op jit(solution)/shard_map/ppermute | solution.py:20
  71.6 2.1 %fusion.7 = (f32[512]{0:T(512)S(1)}, f32[512]{0:T(512)S(1)}) fusion(bf16[512,1024]{1,0:T(8,128)(2,1)S(1)} %fusion.1, bf16[512,1024]{1,0:T(8,128)(2,1)} %collective-permute-done.5), kind=kOutput, calls=%fused_computation.20 | convolution fusion | flops 538704896 | bytes 2101248 | tf_op jit(solution)/shard_map/dot_general | solution.py:32
  73.8 3.7 %collective-permute-done.6 = bf16[512,1024]{1,0:T(8,128)(2,1)S(1)} collective-permute-done((bf16[512,1024]{1,0:T(8,128)(2,1)S(1)}, bf16[512,1024]{1,0:T(8,128)(2,1)S(1)}, u32[]{:S(2)}, u32[]{:S(2)}) %collective-permute-start.6) | collective-permute-done | bytes 1048608 | tf_op jit(solution)/shard_map/ppermute | solution.py:20
  77.5 0.9 fusion.8
  78.4 0.1 collective-permute-done
  78.5 0.9 fusion.2
  79.5 1.4 %collective-permute-done.1 = bf16[512,1024]{1,0:T(8,128)(2,1)S(1)} collective-permute-done((bf16[512,1024]{1,0:T(8,128)(2,1)S(1)}, bf16[512,1024]{1,0:T(8,128)(2,1)S(1)}, u32[]{:S(2)}, u32[]{:S(2)}) %collective-permute-start.1) | collective-permute-done | bytes 1048608 | tf_op jit(solution)/shard_map/ppermute | solution.py:20
  80.8 0.9 fusion.3
  81.7 37.1 %collective-permute-done.2 = bf16[512,1024]{1,0:T(8,128)(2,1)S(1)} collective-permute-done((bf16[512,1024]{1,0:T(8,128)(2,1)S(1)}, bf16[512,1024]{1,0:T(8,128)(2,1)S(1)}, u32[]{:S(2)}, u32[]{:S(2)}) %collective-permute-start.2) | collective-permute-done | bytes 1048608 | tf_op jit(solution)/shard_map/ppermute | solution.py:20
  118.8 0.9 fusion.4
  119.8 0.0 collective-permute-done.7
  119.8 0.9 fusion.9
  120.7 0.6 select_add_fusion
  121.3 0.6 maximum_maximum_fusion
  (3 shorter events, 0.1 us)
Async XLA Ops:
  0.6 1.6 %copy-start = (bf16[512,1024]{1,0:T(8,128)(2,1)S(1)}, bf16[512,1024]{1,0:T(8,128)(2,1)}, u32[]{:S(2)}) copy-start(bf16[512,1024]{1,0:T(8,128)(2,1)} %param.2) | copy-start | bytes 3145732
  2.2 18.2 %copy-start.1 = (s32[170]{0:T(256)S(1)}, s32[170]{0:T(256)}, u32[]{:S(2)}) copy-start(s32[170]{0:T(256)} %param.3) | copy-start | bytes 2044
  2.5 51.5 %collective-permute-start.3 = (bf16[512,1024]{1,0:T(8,128)(2,1)S(1)}, bf16[512,1024]{1,0:T(8,128)(2,1)}, u32[]{:S(2)}, u32[]{:S(2)}) collective-permute-start(bf16[512,1024]{1,0:T(8,128)(2,1)S(1)} %fusion.1), channel_id=1, source_target_pairs={{2,0},{3,1},{4,2},{5,3},{6,4},{7,5},{8,6},{9,7},{10,8},{11,9},{12,... | collective-permute-start | bytes 3145736 | tf_op jit(solution)/shard_map/ppermute | solution.py:20
  7.0 52.1 %collective-permute-start.4 = (bf16[512,1024]{1,0:T(8,128)(2,1)S(1)}, bf16[512,1024]{1,0:T(8,128)(2,1)}, u32[]{:S(2)}, u32[]{:S(2)}) collective-permute-start(bf16[512,1024]{1,0:T(8,128)(2,1)S(1)} %fusion.1), channel_id=1, source_target_pairs={{0,3},{1,4},{2,5},{3,6},{4,7},{5,8},{6,9},{7,10},{8,11},{9,12},{10... | collective-permute-start | bytes 3145736 | tf_op jit(solution)/shard_map/ppermute | solution.py:20
  11.7 57.0 %collective-permute-start.5 = (bf16[512,1024]{1,0:T(8,128)(2,1)S(1)}, bf16[512,1024]{1,0:T(8,128)(2,1)}, u32[]{:S(2)}, u32[]{:S(2)}) collective-permute-start(bf16[512,1024]{1,0:T(8,128)(2,1)S(1)} %fusion.1), channel_id=1, source_target_pairs={{3,0},{4,1},{5,2},{6,3},{7,4},{8,5},{9,6},{10,7},{11,8},{12,9},{13... | collective-permute-start | bytes 3145736 | tf_op jit(solution)/shard_map/ppermute | solution.py:20
  13.8 63.8 %collective-permute-start.6 = (bf16[512,1024]{1,0:T(8,128)(2,1)S(1)}, bf16[512,1024]{1,0:T(8,128)(2,1)S(1)}, u32[]{:S(2)}, u32[]{:S(2)}) collective-permute-start(bf16[512,1024]{1,0:T(8,128)(2,1)S(1)} %fusion.1), channel_id=1, source_target_pairs={{0,4},{1,5},{2,6},{3,7},{4,8},{5,9},{6,10},{7,11},{8,12},{9,13},{1... | collective-permute-start | bytes 3145736 | tf_op jit(solution)/shard_map/ppermute | solution.py:20
  18.5 60.0 %collective-permute-start = (bf16[512,1024]{1,0:T(8,128)(2,1)S(1)}, bf16[512,1024]{1,0:T(8,128)(2,1)S(1)}, u32[]{:S(2)}, u32[]{:S(2)}) collective-permute-start(bf16[512,1024]{1,0:T(8,128)(2,1)S(1)} %fusion.1), channel_id=1, source_target_pairs={{0,1},{1,2},{2,3},{3,4},{4,5},{5,6},{6,7},{7,8},{8,9},{9,10},{10,1... | collective-permute-start | bytes 3145736 | tf_op jit(solution)/shard_map/ppermute | solution.py:20
  54.0 26.8 %collective-permute-start.1 = (bf16[512,1024]{1,0:T(8,128)(2,1)S(1)}, bf16[512,1024]{1,0:T(8,128)(2,1)S(1)}, u32[]{:S(2)}, u32[]{:S(2)}) collective-permute-start(bf16[512,1024]{1,0:T(8,128)(2,1)S(1)} %fusion.1), channel_id=1, source_target_pairs={{1,0},{2,1},{3,2},{4,3},{5,4},{6,5},{7,6},{8,7},{9,8},{10,9},{11,1... | collective-permute-start | bytes 3145736 | tf_op jit(solution)/shard_map/ppermute | solution.py:20
  59.1 59.7 %collective-permute-start.2 = (bf16[512,1024]{1,0:T(8,128)(2,1)S(1)}, bf16[512,1024]{1,0:T(8,128)(2,1)S(1)}, u32[]{:S(2)}, u32[]{:S(2)}) collective-permute-start(bf16[512,1024]{1,0:T(8,128)(2,1)S(1)} %fusion.1), channel_id=1, source_target_pairs={{0,2},{1,3},{2,4},{3,5},{4,6},{5,7},{6,8},{7,9},{8,10},{9,11},{10,... | collective-permute-start | bytes 3145736 | tf_op jit(solution)/shard_map/ppermute | solution.py:20
  68.7 51.0 %collective-permute-start.7 = (bf16[512,1024]{1,0:T(8,128)(2,1)S(1)}, bf16[512,1024]{1,0:T(8,128)(2,1)S(1)}, u32[]{:S(2)}, u32[]{:S(2)}) collective-permute-start(bf16[512,1024]{1,0:T(8,128)(2,1)S(1)} %fusion.1), channel_id=1, source_target_pairs={{4,0},{5,1},{6,2},{7,3},{8,4},{9,5},{10,6},{11,7},{12,8},{13,9},{1... | collective-permute-start | bytes 3145736 | tf_op jit(solution)/shard_map/ppermute | solution.py:20
where the time goes:
time: 122 us
  waiting for transfers between devices  77.8 us (64%)
  starting transfers between devices  25.7 us (21%)
  matrix products  12 us (10%)
  other arithmetic  4.08 us (3%)
  between operations  2.12 us (2%)
    ppermute x8, waiting for transfers between devices, passed_along(): return lax.ppermute(block, axis, route)  77.8 us
    ppermute x8, starting transfers between devices, passed_along(): return lax.ppermute(block, axis, route)  25.7 us
    dot_general x8, matrix products, block_stats(): lax.dot_general(mine_rows, other_rows, (((1,), (1,)), ((), ())), preferre...  11 us
  transfers between devices with their start and end apart: 8, of which 6 were waited for; matrix products, arithmetic and copies ran while one was open for 10% of the time, Pallas kernels for 0%

commit v1 on v0

v1 whole, which is shorter than its diff:
```python
import math

import jax
import jax.numpy as jnp
from jax import lax
from jax.experimental import pallas as pl
from jax.experimental.pallas import tpu as pltpu
from jax.sharding import PartitionSpec as P

MOST = 5
AXES = ("clus", "blk")
RING = 4

epsilon = 1e-06
threshold = 0.5
sharpness = 20.0
floor_value = -2.0

OWN, FIRST, SECOND, BELOW, EDGE = range(5)


def upper_source(p):
    return p - 1 if p % RING else p + RING - 1


def lower_source(p):
    return p + 1 if p % RING else p + RING + 1


def routes(total, line):
    below, first, second, edge, up, down = [], [], [], [], [], []
    for p in range(total):
        if p >= RING:
            below.append((p - RING, p))
        odd_line = (p // line) % 2
        u, d = upper_source(p), lower_source(p)
        up.append((u, p))
        (second if odd_line else first).append((u, p))
        if d < total:
            down.append((d, p))
            if d // line != p // line:
                edge.append((d, p))
            else:
                (first if odd_line else second).append((d, p))
    return below, first, second, edge, up, down


def inverse(route):
    return [(b, a) for a, b in route]


def unitize(values):
    widened = values.astype(jnp.float32)
    factor = lax.rsqrt(jnp.mean(widened * widened, axis=-1, keepdims=True) + epsilon) * (
        1.0 / math.sqrt(values.shape[-1])
    )
    return (widened * factor).astype(jnp.bfloat16)


def closeness_of(scores):
    return 1.0 / (1.0 + jnp.exp(-sharpness * (scores - threshold)))


def fold_rows(part, op):
    width = part.shape[1]
    folded = part[:, :128]
    for k in range(1, width // 128):
        folded = op(folded, part[:, k * 128 : (k + 1) * 128])
    flipped = folded.T
    return flipped


def diag_kernel(x_ref, out_ref):
    rows = x_ref.shape[0]
    step = 128
    for r in range(rows // step):
        scores = lax.dot_general(
            x_ref[r * step : (r + 1) * step, :],
            x_ref[...],
            (((1,), (1,)), ((), ())),
            preferred_element_type=jnp.float32,
        )
        self_pair = (
            lax.broadcasted_iota(jnp.int32, scores.shape, 0) + r * step
            == lax.broadcasted_iota(jnp.int32, scores.shape, 1)
        )
        near = jnp.where(self_pair, 0.0, closeness_of(scores))
        high = jnp.where(self_pair, floor_value, scores)
        span = slice(r * step, (r + 1) * step)
        out_ref[0:1, span] = jnp.max(fold_rows(high, jnp.maximum), axis=0, keepdims=True)
        out_ref[1:2, span] = jnp.sum(fold_rows(near, jnp.add), axis=0, keepdims=True)


def pair_kernel(table_ref, x_ref, a_ref, b_ref, z_ref, e_ref, own_ref, ox_ref, ou_ref, od_ref, oz_ref, slabs, best, count):
    rows = x_ref.shape[0]
    step = 128
    slabs[OWN] = x_ref[...]
    slabs[FIRST] = a_ref[...]
    slabs[SECOND] = b_ref[...]
    slabs[BELOW] = z_ref[...]
    slabs[EDGE] = e_ref[...]
    best[...] = jnp.full(best.shape, floor_value, jnp.float32)
    count[...] = jnp.zeros(count.shape, jnp.float32)

    def one(k, carry):
        i, j = table_ref[2 * k + 1], table_ref[2 * k + 2]

        for r in range(rows // step):
            scores = lax.dot_general(
                slabs[i, r * step : (r + 1) * step, :],
                slabs[j],
                (((1,), (1,)), ((), ())),
                preferred_element_type=jnp.float32,
            )
            near = closeness_of(scores)
            span = slice(r * step, (r + 1) * step)
            tall = (step // 8, 8, rows)
            best[j] = jnp.maximum(best[j], jnp.max(scores.reshape(tall), axis=0))
            count[j] = count[j] + jnp.sum(near.reshape(tall), axis=0)
            high_t = fold_rows(scores, jnp.maximum).reshape(16, 8, step)
            near_t = fold_rows(near, jnp.add).reshape(16, 8, step)
            best[i, :, span] = jnp.maximum(best[i, :, span], jnp.max(high_t, axis=0))
            count[i, :, span] = count[i, :, span] + jnp.sum(near_t, axis=0)
        return carry

    lax.fori_loop(0, table_ref[0], one, 0)

    def emit(ref, slot):
        ref[0:1, :] = jnp.max(best[slot], axis=0, keepdims=True)
        ref[1:2, :] = jnp.sum(count[slot], axis=0, keepdims=True)

    iu, idn = table_ref[11], table_ref[12]
    ox_ref[0:1, :] = jnp.maximum(own_ref[0:1, :], jnp.max(best[OWN], axis=0, keepdims=True))
    ox_ref[1:2, :] = own_ref[1:2, :] + jnp.sum(count[OWN], axis=0, keepdims=True)
    emit(ou_ref, iu)
    emit(od_ref, idn)
    emit(oz_ref, BELOW)


VMEM = pl.BlockSpec(memory_space=pltpu.VMEM)


def pair_stats(table, own_slab, first, second, below, edge, own):
    rows, width = own_slab.shape
    stat = jax.ShapeDtypeStruct((2, rows), jnp.float32)
    return pl.pallas_call(
        pair_kernel,
        in_specs=[pl.BlockSpec(memory_space=pltpu.SMEM)] + [VMEM] * 6,
        out_specs=[VMEM] * 4,
        out_shape=[stat] * 4,
        scratch_shapes=[
            pltpu.VMEM((5, rows, width), jnp.bfloat16),
            pltpu.VMEM((5, 8, rows), jnp.float32),
            pltpu.VMEM((5, 8, rows), jnp.float32),
        ],
        compiler_params=pltpu.CompilerParams(vmem_limit_bytes=40 * 1024 * 1024),
        cost_estimate=pl.CostEstimate(flops=3 * 2 * rows * rows * width, bytes_accessed=5 * rows * width * 2, transcendentals=0),
    )(table, own_slab, first, second, below, edge, own)


def diag_stats(own_slab):
    rows, width = own_slab.shape
    return pl.pallas_call(
        diag_kernel,
        in_specs=[VMEM],
        out_specs=VMEM,
        out_shape=jax.ShapeDtypeStruct((2, rows), jnp.float32),
        compiler_params=pltpu.CompilerParams(vmem_limit_bytes=20 * 1024 * 1024),
        cost_estimate=pl.CostEstimate(flops=2 * rows * rows * width, bytes_accessed=rows * width * 2, transcendentals=0),
    )(own_slab)


def pair_table(cluster_sizes, line, total):
    p = lax.axis_index(AXES)
    x = p % RING
    odd_line = (p // line) % 2
    cluster_end = jnp.cumsum(cluster_sizes)

    def cluster_of(q):
        return jnp.sum((cluster_end <= q).astype(jnp.int32))

    mine = cluster_of(p)
    qu = jnp.where(x == 0, p + RING - 1, p - 1)
    qd = jnp.where(x == 0, p + RING + 1, p + 1)
    qz = p - RING
    cu, cd, cz = cluster_of(qu), cluster_of(qd), cluster_of(qz)
    has_d = qd < total
    has_z = qz >= 0
    iu = jnp.where(odd_line == 1, SECOND, FIRST)
    idn = jnp.where(qd // line != p // line, EDGE, jnp.where(odd_line == 1, FIRST, SECOND))
    wanted = [
        (cu == mine, OWN, iu),
        ((cd == mine) & has_d & (x == RING - 1), OWN, idn),
        ((cu == cd) & has_d, iu, idn),
        ((cz == mine) & has_z, BELOW, OWN),
        ((cz == cu) & has_z & (x > 0), BELOW, iu),
    ]
    flags = jnp.stack([w for w, _, _ in wanted]).astype(jnp.int32)
    order = jnp.cumsum(flags) - 1
    left = jnp.stack([jnp.asarray(i, jnp.int32) for _, i, _ in wanted])
    right = jnp.stack([jnp.asarray(j, jnp.int32) for _, _, j in wanted])
    place = (order[None, :] == jnp.arange(5)[:, None]) & (flags[None, :] == 1)
    left = jnp.sum(jnp.where(place, left[None, :], 0), axis=1)
    right = jnp.sum(jnp.where(place, right[None, :], 0), axis=1)
    pairs = jnp.stack([left, right], axis=1).reshape(-1)
    return jnp.concatenate([jnp.sum(flags)[None], pairs, iu[None], idn[None]]).astype(jnp.int32)


def shards(line, total):
    below_route, first_route, second_route, edge_route, up_route, down_route = routes(total, line)

    def body(embeddings, cluster_sizes):
        normed = unitize(embeddings)
        below = lax.ppermute(normed, AXES, below_route)
        first = lax.ppermute(normed, AXES, first_route)
        second = lax.ppermute(normed, AXES, second_route)
        edge = lax.ppermute(normed, AXES, edge_route)
        own = diag_stats(normed)
        table = pair_table(cluster_sizes, line, total)
        mine, for_up, for_down, for_below = pair_stats(table, normed, first, second, below, edge, own)
        from_down = lax.ppermute(for_down, AXES, inverse(down_route))
        from_up = lax.ppermute(for_up, AXES, inverse(up_route))
        from_below = lax.ppermute(for_below, AXES, inverse(below_route))
        p = lax.axis_index(AXES)
        got_down = p >= 2
        got_below = p < total - RING
        best = jnp.maximum(mine[0], from_up[0])
        best = jnp.maximum(best, jnp.where(got_down, from_down[0], floor_value))
        best = jnp.maximum(best, jnp.where(got_below, from_below[0], floor_value))
        return best, mine[1] + from_up[1] + from_down[1] + from_below[1]

    return body


def solution(mesh):
    line = mesh.shape["blk"]
    total = line * mesh.shape["clus"]
    return jax.shard_map(
        shards(line, total),
        mesh=mesh,
        in_specs=(P(AXES, None), P()),
        out_specs=(P(AXES), P(AXES)),
        check_vma=False,
    )
```

time: 122 us -> 67.4 us (0.55)
  the two profiles are of different devices: /device:TPU:506 before, /device:TPU:9 now
where the time goes in v1:
time: 67.4 us; the launch traced here: 67 us
  starting transfers between devices  38.5 us (57%)
  waiting for transfers between devices  10.2 us (15%)
  between operations  6.99 us (10%)
  Pallas kernels  5.42 us (8%)
  other arithmetic  5.3 us (8%)
  local copies, waits for them, and re-layouts  0.68 us (1%)
    ppermute x1, starting transfers between devices, body(): edge = lax.ppermute(normed, AXES, edge_route)  13.3 us
    ppermute x1, starting transfers between devices, body(): from_below = lax.ppermute(for_below, AXES, inverse(below_route))  9.9 us
    ppermute x1, waiting for transfers between devices, body(): below = lax.ppermute(normed, AXES, below_route)  7.21 us
    ppermute x1, starting transfers between devices, body(): below = lax.ppermute(normed, AXES, below_route)  4.99 us
    ppermute x1, starting transfers between devices, body(): from_up = lax.ppermute(for_up, AXES, inverse(up_route))  3.95 us
    pallas_call x1, Pallas kernels, pair_stats(): pl.pallas_call(pair_kernel, in_specs=[pl.BlockSpec(memory_space=pltpu.SME...  3.71 us
    ppermute x1, starting transfers between devices, body(): second = lax.ppermute(normed, AXES, second_route)  3.12 us
    ppermute x1, waiting for transfers between devices, body(): edge = lax.ppermute(normed, AXES, edge_route)  2.23 us
  transfers between devices with their start and end apart: 7, of which 3 were waited for; matrix products, arithmetic and copies ran while one was open for 5% of the time, Pallas kernels for 3%

profile of v1, /device:TPU:9, one launch (start us, length us, event | category | flops | bytes accessed | tf_op | source)
XLA Modules:
  0.0 67.0 jit_solution(16993478110503232471)
XLA Ops:
  0.6 0.0 copy-start
  0.6 1.6 %fusion = f32[512]{0:T(512)S(1)} fusion(bf16[512,1024]{1,0:T(8,128)(2,1)} %param.2), kind=kLoop, calls=%fused_computation.2 | loop fusion | flops 1572352 | bytes 1050624 | tf_op jit(solution)/shard_map/reduce_sum | solution.py:54
  2.2 0.0 copy-done
  2.2 0.0 copy-start.1
  2.3 0.2 fusion.1.x_ref
  2.5 1.3 %collective-permute-start = (bf16[512,1024]{1,0:T(8,128)(2,1)S(1)}, bf16[512,1024]{1,0:T(8,128)(2,1)S(1)}, u32[]{:S(2)}, u32[]{:S(2)}) collective-permute-start(bf16[512,1024]{1,0:T(8,128)(2,1)S(1)} %fusion.1.x_ref), channel_id=1, source_target_pairs={{3,0},{0,1},{1,2},{2,3},{7,4},{4,5},{5,6},{6,7},{11,8},{8,9},{9,10... | collective-permute-start | bytes 3145736 | tf_op jit(solution)/shard_map/ppermute | solution.py:215
  3.8 3.1 %collective-permute-start.1 = (bf16[512,1024]{1,0:T(8,128)(2,1)S(1)}, bf16[512,1024]{1,0:T(8,128)(2,1)S(1)}, u32[]{:S(2)}, u32[]{:S(2)}) collective-permute-start(bf16[512,1024]{1,0:T(8,128)(2,1)S(1)} %fusion.1.x_ref), channel_id=1, source_target_pairs={{5,0},{2,1},{3,2},{4,3},{9,4},{6,5},{7,6},{8,7},{13,8},{10,9},{11,... | collective-permute-start | bytes 3145736 | tf_op jit(solution)/shard_map/ppermute | solution.py:216
  6.9 5.0 %collective-permute-start.2 = (bf16[512,1024]{1,0:T(8,128)(2,1)S(1)}, bf16[512,1024]{1,0:T(8,128)(2,1)}, u32[]{:S(2)}, u32[]{:S(2)}) collective-permute-start(bf16[512,1024]{1,0:T(8,128)(2,1)S(1)} %fusion.1.x_ref), channel_id=1, source_target_pairs={{0,4},{1,5},{2,6},{3,7},{4,8},{5,9},{6,10},{7,11},{8,12},{9,13},{1... | collective-permute-start | bytes 3145736 | tf_op jit(solution)/shard_map/ppermute | solution.py:214
  11.9 13.3 %collective-permute-start.3 = (bf16[512,1024]{1,0:T(8,128)(2,1)S(1)}, bf16[512,1024]{1,0:T(8,128)(2,1)}, u32[]{:S(2)}, u32[]{:S(2)}) collective-permute-start(bf16[512,1024]{1,0:T(8,128)(2,1)S(1)} %fusion.1.x_ref), channel_id=1, source_target_pairs={{65,60},{64,63},{129,124},{128,127},{193,188},{192,191},{257,252},... | collective-permute-start | bytes 3145736 | tf_op jit(solution)/shard_map/ppermute | solution.py:217
  25.3 0.0 copy-done.1
  25.3 0.3 reduce-window.19
  25.6 0.1 slice.34
  25.7 0.1 slice_reduce_fusion
  25.8 0.1 add_bitcast_fusion
  25.9 0.7 %fusion.8 = (s32[]{:T(128)}, s32[]{:T(128)}, s32[]{:T(128)}, s32[]{:T(128)}) fusion(s32[]{:T(128)S(6)} %sub.24, s32[256]{0:T(256)S(1)} %add_bitcast_fusion, s32[]{:T(128)S(6)} %add.61, s32[]{:T(128)S(6)} %select_n.61, s32[]{:T(128)S(6)} %select_n.60), kind=kLoop, calls=%fused_computation.24 | loop fusion | flops 2036 | bytes 712 | tf_op jit(solution)/shard_map/reduce_sum | solution.py:180
  32.8 0.1 stack.65
  32.9 0.2 reduce-window.21
  33.1 0.1 stack.70
  33.2 0.1 stack.59
  33.3 0.1 pad_add_fusion.1
  33.4 0.1 select_reduce_fusion.1
  33.5 0.1 copy.6
  33.6 0.1 reshape.194
  33.7 1.7 %shard_map.41.own_ref = f32[2,512]{1,0:T(2,128)S(1)} custom-call(bf16[512,1024]{1,0:T(8,128)(2,1)S(1)} %fusion.1.x_ref), custom_call_target="tpu_custom_call" | custom-call | flops 536870912 | bytes 1048576 | tf_op jit(solution)/shard_map/pallas_call | solution.py:163
  35.4 0.6 convert_reduce_fusion
  36.1 0.7 %pad_add_fusion.2.table_ref = s32[13]{0:T(128)S(1)} fusion(s32[1]{0:T(128)} %bitcast.16, s32[1]{0:T(128)} %bitcast.14, s32[10]{0:T(128)S(1)} %reshape.194, s32[1]{0:T(128)} %bitcast.7), kind=kLoop, calls=%fused_computation.30 | loop fusion | flops 39 | bytes 104 | tf_op jit(solution)/shard_map/concatenate | solution.py:206
  36.8 0.0 collective-permute-done.a_ref
  36.8 0.0 collective-permute-done.1.b_ref
  36.8 7.2 %collective-permute-done.2.z_ref = bf16[512,1024]{1,0:T(8,128)(2,1)} collective-permute-done((bf16[512,1024]{1,0:T(8,128)(2,1)S(1)}, bf16[512,1024]{1,0:T(8,128)(2,1)}, u32[]{:S(2)}, u32[]{:S(2)}) %collective-permute-start.2) | collective-permute-done | bytes 1048608 | tf_op jit(solution)/shard_map/ppermute | solution.py:214
  44.0 2.2 %collective-permute-done.3.e_ref = bf16[512,1024]{1,0:T(8,128)(2,1)} collective-permute-done((bf16[512,1024]{1,0:T(8,128)(2,1)S(1)}, bf16[512,1024]{1,0:T(8,128)(2,1)}, u32[]{:S(2)}, u32[]{:S(2)}) %collective-permute-start.3) | collective-permute-done | bytes 1048608 | tf_op jit(solution)/shard_map/ppermute | solution.py:217
  46.2 3.7 %shard_map.42 = (f32[2,512]{1,0:T(2,128)S(1)}, f32[2,512]{1,0:T(2,128)S(1)}, f32[2,512]{1,0:T(2,128)S(1)}, f32[2,512]{1,0:T(2,128)S(1)}) custom-call(s32[13]{0:T(128)S(1)} %pad_add_fusion.2.table_ref, bf16[512,1024]{1,0:T(8,128)(2,1)S(1)} %fusion.1.x_ref, bf16[512,1024]{1,0:T(8,128)(2,1)S(1)} %collective-permute-done.a_ref, ...), custom_call_target="tpu_custom_call" | custom-call | flops 1610612736 | bytes 5242880 | tf_op jit(solution)/shard_map/pallas_call | solution.py:146
  49.9 3.9 %collective-permute-start.4 = (f32[2,512]{1,0:T(2,128)S(1)}, f32[2,512]{1,0:T(2,128)S(1)}, u32[]{:S(2)}, u32[]{:S(2)}) collective-permute-start(f32[2,512]{1,0:T(2,128)S(1)} %get-tuple-element.7), channel_id=1, source_target_pairs={{0,3},{1,0},{2,1},{3,2},{4,7},{5,4},{6,5},{7,6},{8,11},{9,8},{10,9... | collective-permute-start | bytes 12296 | tf_op jit(solution)/shard_map/ppermute | solution.py:222
  53.9 1.9 %collective-permute-start.5 = (f32[2,512]{1,0:T(2,128)S(1)}, f32[2,512]{1,0:T(2,128)S(1)}, u32[]{:S(2)}, u32[]{:S(2)}) collective-permute-start(f32[2,512]{1,0:T(2,128)S(1)} %get-tuple-element.8), channel_id=1, source_target_pairs={{0,5},{1,2},{2,3},{3,4},{4,9},{5,6},{6,7},{7,8},{8,13},{9,10},{10,... | collective-permute-start | bytes 12296 | tf_op jit(solution)/shard_map/ppermute | solution.py:221
  55.8 9.9 %collective-permute-start.6 = (f32[2,512]{1,0:T(2,128)S(1)}, f32[2,512]{1,0:T(2,128)S(1)}, u32[]{:S(2)}, u32[]{:S(2)}) collective-permute-start(f32[2,512]{1,0:T(2,128)S(1)} %get-tuple-element.9), channel_id=1, source_target_pairs={{4,0},{5,1},{6,2},{7,3},{8,4},{9,5},{10,6},{11,7},{12,8},{13,9},{1... | collective-permute-start | bytes 12296 | tf_op jit(solution)/shard_map/ppermute | solution.py:223
  65.7 0.0 collective-permute-done.4
  65.7 0.0 collective-permute-done.5
  65.7 0.7 %collective-permute-done.6 = f32[2,512]{1,0:T(2,128)S(1)} collective-permute-done((f32[2,512]{1,0:T(2,128)S(1)}, f32[2,512]{1,0:T(2,128)S(1)}, u32[]{:S(2)}, u32[]{:S(2)}) %collective-permute-start.6) | collective-permute-done | bytes 4128 | tf_op jit(solution)/shard_map/ppermute | solution.py:223
  66.5 0.6 slice_add_fusion
  (9 shorter events, 0.1 us)
Async XLA Ops:
  0.6 1.6 %copy-start = (bf16[512,1024]{1,0:T(8,128)(2,1)S(1)}, bf16[512,1024]{1,0:T(8,128)(2,1)}, u32[]{:S(2)}) copy-start(bf16[512,1024]{1,0:T(8,128)(2,1)} %param.2) | copy-start | bytes 3145732
  2.2 23.0 %copy-start.1 = (s32[170]{0:T(256)S(1)}, s32[170]{0:T(256)}, u32[]{:S(2)}) copy-start(s32[170]{0:T(256)} %param.3) | copy-start | bytes 2044
  2.5 34.3 %collective-permute-start = (bf16[512,1024]{1,0:T(8,128)(2,1)S(1)}, bf16[512,1024]{1,0:T(8,128)(2,1)S(1)}, u32[]{:S(2)}, u32[]{:S(2)}) collective-permute-start(bf16[512,1024]{1,0:T(8,128)(2,1)S(1)} %fusion.1.x_ref), channel_id=1, source_target_pairs={{3,0},{0,1},{1,2},{2,3},{7,4},{4,5},{5,6},{6,7},{11,8},{8,9},{9,10... | collective-permute-start | bytes 3145736 | tf_op jit(solution)/shard_map/ppermute | solution.py:215
  3.8 33.0 %collective-permute-start.1 = (bf16[512,1024]{1,0:T(8,128)(2,1)S(1)}, bf16[512,1024]{1,0:T(8,128)(2,1)S(1)}, u32[]{:S(2)}, u32[]{:S(2)}) collective-permute-start(bf16[512,1024]{1,0:T(8,128)(2,1)S(1)} %fusion.1.x_ref), channel_id=1, source_target_pairs={{5,0},{2,1},{3,2},{4,3},{9,4},{6,5},{7,6},{8,7},{13,8},{10,9},{11,... | collective-permute-start | bytes 3145736 | tf_op jit(solution)/shard_map/ppermute | solution.py:216
  6.9 37.0 %collective-permute-start.2 = (bf16[512,1024]{1,0:T(8,128)(2,1)S(1)}, bf16[512,1024]{1,0:T(8,128)(2,1)}, u32[]{:S(2)}, u32[]{:S(2)}) collective-permute-start(bf16[512,1024]{1,0:T(8,128)(2,1)S(1)} %fusion.1.x_ref), channel_id=1, source_target_pairs={{0,4},{1,5},{2,6},{3,7},{4,8},{5,9},{6,10},{7,11},{8,12},{9,13},{1... | collective-permute-start | bytes 3145736 | tf_op jit(solution)/shard_map/ppermute | solution.py:214
  11.9 34.3 %collective-permute-start.3 = (bf16[512,1024]{1,0:T(8,128)(2,1)S(1)}, bf16[512,1024]{1,0:T(8,128)(2,1)}, u32[]{:S(2)}, u32[]{:S(2)}) collective-permute-start(bf16[512,1024]{1,0:T(8,128)(2,1)S(1)} %fusion.1.x_ref), channel_id=1, source_target_pairs={{65,60},{64,63},{129,124},{128,127},{193,188},{192,191},{257,252},... | collective-permute-start | bytes 3145736 | tf_op jit(solution)/shard_map/ppermute | solution.py:217
  49.9 15.8 %collective-permute-start.4 = (f32[2,512]{1,0:T(2,128)S(1)}, f32[2,512]{1,0:T(2,128)S(1)}, u32[]{:S(2)}, u32[]{:S(2)}) collective-permute-start(f32[2,512]{1,0:T(2,128)S(1)} %get-tuple-element.7), channel_id=1, source_target_pairs={{0,3},{1,0},{2,1},{3,2},{4,7},{5,4},{6,5},{7,6},{8,11},{9,8},{10,9... | collective-permute-start | bytes 12296 | tf_op jit(solution)/shard_map/ppermute | solution.py:222
  53.9 11.9 %collective-permute-start.5 = (f32[2,512]{1,0:T(2,128)S(1)}, f32[2,512]{1,0:T(2,128)S(1)}, u32[]{:S(2)}, u32[]{:S(2)}) collective-permute-start(f32[2,512]{1,0:T(2,128)S(1)} %get-tuple-element.8), channel_id=1, source_target_pairs={{0,5},{1,2},{2,3},{3,4},{4,9},{5,6},{6,7},{7,8},{8,13},{9,10},{10,... | collective-permute-start | bytes 12296 | tf_op jit(solution)/shard_map/ppermute | solution.py:221
  55.8 10.6 %collective-permute-start.6 = (f32[2,512]{1,0:T(2,128)S(1)}, f32[2,512]{1,0:T(2,128)S(1)}, u32[]{:S(2)}, u32[]{:S(2)}) collective-permute-start(f32[2,512]{1,0:T(2,128)S(1)} %get-tuple-element.9), channel_id=1, source_target_pairs={{4,0},{5,1},{6,2},{7,3},{8,4},{9,5},{10,6},{11,7},{12,8},{13,9},{1... | collective-permute-start | bytes 12296 | tf_op jit(solution)/shard_map/ppermute | solution.py:223

commit v2 on v1

v2 whole, which is shorter than its diff:
```python
import functools
import math

import jax
import jax.numpy as jnp
from jax import lax
from jax.experimental import pallas as pl
from jax.experimental.pallas import tpu as pltpu
from jax.sharding import PartitionSpec as P

MOST = 5
AXES = ("clus", "blk")
RING = 4

epsilon = 1e-06
threshold = 0.5
sharpness = 20.0
floor_value = -2.0

SLOTS = 5
OWN, FIRST, SECOND, BELOW, EDGE = range(SLOTS)
AT_U, AT_D, USED = 13, 14, 16
TABLE = 32
LANES = 128
TILE = 256


def upper_source(p):
    return p - 1 if p % RING else p + RING - 1


def lower_source(p):
    return p + 1 if p % RING else p + RING + 1


def routes(total, line):
    below, first, second, edge, up, down = [], [], [], [], [], []
    for p in range(total):
        if p >= RING:
            below.append((p - RING, p))
        odd_line = (p // line) % 2
        u, d = upper_source(p), lower_source(p)
        up.append((u, p))
        (second if odd_line else first).append((u, p))
        if d < total:
            down.append((d, p))
            if d // line != p // line:
                edge.append((d, p))
            else:
                (first if odd_line else second).append((d, p))
    return below, first, second, edge, up, down


def inverse(route):
    return [(b, a) for a, b in route]


def unitize(values):
    widened = values.astype(jnp.float32)
    factor = lax.rsqrt(jnp.mean(widened * widened, axis=-1, keepdims=True) + epsilon) * (
        1.0 / math.sqrt(values.shape[-1])
    )
    return (widened * factor).astype(jnp.bfloat16)


def closeness_of(scores):
    return jax.nn.sigmoid(sharpness * (scores - threshold))


def score_block(rows, cols):
    return lax.dot_general(rows, cols, (((1,), (1,)), ((), ())), preferred_element_type=jnp.float32)


def fold_lanes(part, op):
    folded = part[:, :LANES]
    for k in range(1, part.shape[1] // LANES):
        folded = op(folded, part[:, k * LANES : (k + 1) * LANES])
    return folded


def fold_sublanes(part, reduce):
    return reduce(part.reshape(part.shape[0] // 8, 8, part.shape[1]), axis=0)


def write_table(line, total, sizes_ref, place_ref, table_ref):
    p = place_ref[0]
    x = lax.rem(p, RING)
    my_line = lax.div(p, line)
    odd_line = lax.rem(my_line, 2)
    qu = jnp.where(x == 0, p + RING - 1, p - 1)
    qd = jnp.where(x == 0, p + RING + 1, p + 1)
    qz = p - RING

    def step(k, carry):
        end, at_p, at_u, at_d, at_z = carry
        end = end + sizes_ref[k]
        one = jnp.int32(1)
        zero = jnp.int32(0)
        return (
            end,
            at_p + jnp.where(end <= p, one, zero),
            at_u + jnp.where(end <= qu, one, zero),
            at_d + jnp.where(end <= qd, one, zero),
            at_z + jnp.where(end <= qz, one, zero),
        )

    nought = jnp.int32(0)
    _, mine, cu, cd, cz = lax.fori_loop(0, sizes_ref.shape[0], step, (nought,) * 5)
    has_d = qd < total
    has_z = qz >= 0
    iu = jnp.where(odd_line == 1, SECOND, FIRST)
    idn = jnp.where(lax.div(qd, line) != my_line, EDGE, jnp.where(odd_line == 1, FIRST, SECOND))
    wanted = [
        ((cz == mine) & has_z, BELOW, OWN),
        ((cz == cu) & has_z & (x > 0), BELOW, iu),
        (cu == mine, OWN, iu),
        ((cd == mine) & has_d & (x == RING - 1), OWN, idn),
        ((cu == cd) & has_d, iu, idn),
    ]
    n = jnp.int32(0)
    for slot in range(SLOTS):
        table_ref[USED + slot] = 0
    for flag, i, j in wanted:
        table_ref[1 + 2 * n] = jnp.asarray(i, jnp.int32)
        table_ref[2 + 2 * n] = jnp.asarray(j, jnp.int32)
        bit = jnp.where(flag, jnp.int32(1), jnp.int32(0))
        table_ref[USED + i] = jnp.maximum(table_ref[USED + i], bit)
        table_ref[USED + j] = jnp.maximum(table_ref[USED + j], bit)
        n = n + bit
    table_ref[0] = n
    table_ref[AT_U] = jnp.asarray(iu, jnp.int32)
    table_ref[AT_D] = jnp.asarray(idn, jnp.int32)


def diag_kernel(line, total, sizes_ref, place_ref, x_ref, out_ref, table_ref):
    rows = x_ref.shape[0]
    for c in range(rows // TILE):
        span = slice(c * TILE, (c + 1) * TILE)
        scores = score_block(x_ref[...], x_ref[span, :])
        self_pair = lax.broadcasted_iota(jnp.int32, scores.shape, 0) == (
            lax.broadcasted_iota(jnp.int32, scores.shape, 1) + c * TILE
        )
        near = jnp.where(self_pair, 0.0, closeness_of(scores))
        high = jnp.where(self_pair, floor_value, scores)
        out_ref[0:1, span] = jnp.max(high, axis=0, keepdims=True)
        out_ref[1:2, span] = jnp.sum(near, axis=0, keepdims=True)
    write_table(line, total, sizes_ref, place_ref, table_ref)


def pair_kernel(table_ref, own_ref, z_ref, a_ref, b_ref, e_ref, x_ref, ox_ref, ou_ref, od_ref, oz_ref, slabs, best, count, sems):
    held = [(OWN, x_ref), (FIRST, a_ref), (SECOND, b_ref), (BELOW, z_ref), (EDGE, e_ref)]
    rows = slabs.shape[1]
    for slot, ref in held:

        @pl.when(table_ref[USED + slot] == 1)
        def _():
            pltpu.make_async_copy(ref, slabs.at[slot], sems.at[slot]).start()

    best[...] = jnp.full(best.shape, floor_value, jnp.float32)
    count[...] = jnp.zeros(count.shape, jnp.float32)
    for slot, ref in held:

        @pl.when(table_ref[USED + slot] == 1)
        def _():
            pltpu.make_async_copy(ref, slabs.at[slot], sems.at[slot]).wait()

    def one(k, carry):
        i, j = table_ref[2 * k + 1], table_ref[2 * k + 2]
        high_rows = near_rows = None
        for c in range(rows // TILE):
            span = slice(c * TILE, (c + 1) * TILE)
            scores = score_block(slabs[i], slabs[j, span, :])
            near = closeness_of(scores)
            best[j, :, span] = jnp.maximum(best[j, :, span], fold_sublanes(scores, jnp.max))
            count[j, :, span] = count[j, :, span] + fold_sublanes(near, jnp.sum)
            high_part, near_part = fold_lanes(scores, jnp.maximum), fold_lanes(near, jnp.add)
            high_rows = high_part if high_rows is None else jnp.maximum(high_rows, high_part)
            near_rows = near_part if near_rows is None else near_rows + near_part
        best[i] = jnp.maximum(best[i], fold_sublanes(high_rows.T, jnp.max))
        count[i] = count[i] + fold_sublanes(near_rows.T, jnp.sum)
        return carry

    lax.fori_loop(0, table_ref[0], one, 0)

    def emit(ref, slot):
        ref[0:1, :] = jnp.max(best[slot], axis=0, keepdims=True)
        ref[1:2, :] = jnp.sum(count[slot], axis=0, keepdims=True)

    ox_ref[0:1, :] = jnp.maximum(own_ref[0:1, :], jnp.max(best[OWN], axis=0, keepdims=True))
    ox_ref[1:2, :] = own_ref[1:2, :] + jnp.sum(count[OWN], axis=0, keepdims=True)
    emit(ou_ref, table_ref[AT_U])
    emit(od_ref, table_ref[AT_D])
    emit(oz_ref, BELOW)


VMEM = pl.BlockSpec(memory_space=pltpu.VMEM)
SMEM = pl.BlockSpec(memory_space=pltpu.SMEM)
ANY = pl.BlockSpec(memory_space=pl.ANY)


def pair_stats(table, own, below, first, second, edge, own_slab):
    rows, width = own_slab.shape
    stat = jax.ShapeDtypeStruct((2, rows), jnp.float32)
    return pl.pallas_call(
        pair_kernel,
        in_specs=[SMEM, VMEM] + [ANY] * 5,
        out_specs=[VMEM] * 4,
        out_shape=[stat] * 4,
        scratch_shapes=[
            pltpu.VMEM((SLOTS, rows, width), jnp.bfloat16),
            pltpu.VMEM((SLOTS, 8, rows), jnp.float32),
            pltpu.VMEM((SLOTS, 8, rows), jnp.float32),
            pltpu.SemaphoreType.DMA((SLOTS,)),
        ],
        compiler_params=pltpu.CompilerParams(vmem_limit_bytes=24 * 1024 * 1024),
        cost_estimate=pl.CostEstimate(flops=3 * 2 * rows * rows * width, bytes_accessed=5 * rows * width * 2, transcendentals=0),
    )(table, own, below, first, second, edge, own_slab)


def diag_stats(line, total, cluster_sizes, place, own_slab):
    rows, width = own_slab.shape
    return pl.pallas_call(
        functools.partial(diag_kernel, line, total),
        in_specs=[SMEM, SMEM, VMEM],
        out_specs=[VMEM, SMEM],
        out_shape=[
            jax.ShapeDtypeStruct((2, rows), jnp.float32),
            jax.ShapeDtypeStruct((TABLE,), jnp.int32),
        ],
        compiler_params=pltpu.CompilerParams(vmem_limit_bytes=16 * 1024 * 1024),
        cost_estimate=pl.CostEstimate(flops=2 * rows * rows * width, bytes_accessed=rows * width * 2, transcendentals=0),
    )(cluster_sizes, place, own_slab)


def shards(line, total):
    below_route, first_route, second_route, edge_route, up_route, down_route = routes(total, line)

    def body(embeddings, cluster_sizes):
        normed = unitize(embeddings)
        below = lax.ppermute(normed, AXES, below_route)
        first = lax.ppermute(normed, AXES, first_route)
        second = lax.ppermute(normed, AXES, second_route)
        edge = lax.ppermute(normed, AXES, edge_route)
        p = lax.axis_index(AXES)
        own, table = diag_stats(line, total, cluster_sizes, p[None].astype(jnp.int32), normed)
        mine, for_up, for_down, for_below = pair_stats(table, own, below, first, second, edge, normed)
        from_down = lax.ppermute(for_down, AXES, inverse(down_route))
        from_up = lax.ppermute(for_up, AXES, inverse(up_route))
        from_below = lax.ppermute(for_below, AXES, inverse(below_route))
        got_down = p >= 2
        got_below = p < total - RING
        best = jnp.maximum(mine[0], from_up[0])
        best = jnp.maximum(best, jnp.where(got_down, from_down[0], floor_value))
        best = jnp.maximum(best, jnp.where(got_below, from_below[0], floor_value))
        return best, mine[1] + from_up[1] + from_down[1] + from_below[1]

    return body


def solution(mesh):
    line = mesh.shape["blk"]
    total = line * mesh.shape["clus"]
    return jax.shard_map(
        shards(line, total),
        mesh=mesh,
        in_specs=(P(AXES, None), P()),
        out_specs=(P(AXES), P(AXES)),
        check_vma=False,
    )
```

time: 67.4 us -> 67.2 us (level)
  the two profiles are of different devices: /device:TPU:9 before, /device:TPU:16 now
where the time goes in v2:
time: 67.2 us; the launch traced here: 66.9 us
  starting transfers between devices  40.1 us (60%)
  waiting for transfers between devices  18.6 us (28%)
  Pallas kernels  5.04 us (8%)
  other arithmetic  2.43 us (4%)
  between operations  0.75 us (1%)
    ppermute x1, starting transfers between devices, body(): edge = lax.ppermute(normed, AXES, edge_route)  15.1 us
    ppermute x1, starting transfers between devices, body(): from_below = lax.ppermute(for_below, AXES, inverse(below_route))  12.7 us
    ppermute x1, waiting for transfers between devices, body(): edge = lax.ppermute(normed, AXES, edge_route)  11.7 us
    ppermute x1, waiting for transfers between devices, body(): below = lax.ppermute(normed, AXES, below_route)  5.62 us
    pallas_call x1, Pallas kernels, diag_stats(): pl.pallas_call(functools.partial(diag_kernel, line, total), in_specs=[SME...  4.36 us
    ppermute x1, starting transfers between devices, body(): below = lax.ppermute(normed, AXES, below_route)  3.83 us
    ppermute x1, starting transfers between devices, body(): first = lax.ppermute(normed, AXES, first_route)  3.4 us
    ppermute x1, starting transfers between devices, body(): from_up = lax.ppermute(for_up, AXES, inverse(up_route))  1.92 us
  transfers between devices with their start and end apart: 7, of which 3 were waited for; matrix products, arithmetic and copies ran while one was open for 0% of the time, Pallas kernels for 7%

profile of v2, /device:TPU:16, one launch (start us, length us, event | category | flops | bytes accessed | tf_op | source)
XLA Modules:
  0.0 66.9 jit_solution(9538054198664577647)
XLA Ops:
  0.6 0.0 copy-start.1
  0.6 1.6 %fusion = f32[512]{0:T(512)S(1)} fusion(bf16[512,1024]{1,0:T(8,128)(2,1)} %param.2), kind=kLoop, calls=%fused_computation.2 | loop fusion | flops 1572352 | bytes 1050624 | tf_op jit(solution)/shard_map/reduce_sum | solution.py:60
  2.2 0.0 copy-done.1
  2.2 0.0 copy-start
  2.3 0.2 fusion.1.x_ref
  2.5 3.8 %collective-permute-start = (bf16[512,1024]{1,0:T(8,128)(2,1)S(1)}, bf16[512,1024]{1,0:T(8,128)(2,1)S(1)}, u32[]{:S(2)}, u32[]{:S(2)}) collective-permute-start(bf16[512,1024]{1,0:T(8,128)(2,1)S(1)} %fusion.1.x_ref), channel_id=1, source_target_pairs={{0,4},{1,5},{2,6},{3,7},{4,8},{5,9},{6,10},{7,11},{8,12},{9,13},{1... | collective-permute-start | bytes 3145736 | tf_op jit(solution)/shard_map/ppermute | solution.py:240
  6.3 3.4 %collective-permute-start.1 = (bf16[512,1024]{1,0:T(8,128)(2,1)S(1)}, bf16[512,1024]{1,0:T(8,128)(2,1)S(1)}, u32[]{:S(2)}, u32[]{:S(2)}) collective-permute-start(bf16[512,1024]{1,0:T(8,128)(2,1)S(1)} %fusion.1.x_ref), channel_id=1, source_target_pairs={{3,0},{0,1},{1,2},{2,3},{7,4},{4,5},{5,6},{6,7},{11,8},{8,9},{9,10... | collective-permute-start | bytes 3145736 | tf_op jit(solution)/shard_map/ppermute | solution.py:241
  9.7 1.3 %collective-permute-start.2 = (bf16[512,1024]{1,0:T(8,128)(2,1)S(1)}, bf16[512,1024]{1,0:T(8,128)(2,1)}, u32[]{:S(2)}, u32[]{:S(2)}) collective-permute-start(bf16[512,1024]{1,0:T(8,128)(2,1)S(1)} %fusion.1.x_ref), channel_id=1, source_target_pairs={{5,0},{2,1},{3,2},{4,3},{9,4},{6,5},{7,6},{8,7},{13,8},{10,9},{11,... | collective-permute-start | bytes 3145736 | tf_op jit(solution)/shard_map/ppermute | solution.py:242
  11.0 15.1 %collective-permute-start.3 = (bf16[512,1024]{1,0:T(8,128)(2,1)S(1)}, bf16[512,1024]{1,0:T(8,128)(2,1)}, u32[]{:S(2)}, u32[]{:S(2)}) collective-permute-start(bf16[512,1024]{1,0:T(8,128)(2,1)S(1)} %fusion.1.x_ref), channel_id=1, source_target_pairs={{65,60},{64,63},{129,124},{128,127},{193,188},{192,191},{257,252},... | collective-permute-start | bytes 3145736 | tf_op jit(solution)/shard_map/ppermute | solution.py:243
  26.1 0.0 copy-done
  26.1 4.4 %shard_map.41 = (f32[2,512]{1,0:T(2,128)S(1)}, s32[32]{0:T(128)S(1)}) custom-call(s32[170]{0:T(256)S(1)} %copy-done, s32[1]{0:T(128)} %bitcast.place_ref, bf16[512,1024]{1,0:T(8,128)(2,1)S(1)} %fusion.1.x_ref), custom_call_target="tpu_custom_call" | custom-call | flops 536870912 | bytes 1048576 | tf_op jit(solution)/shard_map/pallas_call | solution.py:222
  30.5 5.6 %collective-permute-done.z_ref = bf16[512,1024]{1,0:T(8,128)(2,1)S(1)} collective-permute-done((bf16[512,1024]{1,0:T(8,128)(2,1)S(1)}, bf16[512,1024]{1,0:T(8,128)(2,1)S(1)}, u32[]{:S(2)}, u32[]{:S(2)}) %collective-permute-start) | collective-permute-done | bytes 1048608 | tf_op jit(solution)/shard_map/ppermute | solution.py:240
  36.1 0.0 collective-permute-done.1.a_ref
  36.1 0.0 collective-permute-done.2.b_ref
  36.1 11.7 %collective-permute-done.3.e_ref = bf16[512,1024]{1,0:T(8,128)(2,1)} collective-permute-done((bf16[512,1024]{1,0:T(8,128)(2,1)S(1)}, bf16[512,1024]{1,0:T(8,128)(2,1)}, u32[]{:S(2)}, u32[]{:S(2)}) %collective-permute-start.3) | collective-permute-done | bytes 1048608 | tf_op jit(solution)/shard_map/ppermute | solution.py:243
  47.8 0.7 %shard_map.42 = (f32[2,512]{1,0:T(2,128)S(1)}, f32[2,512]{1,0:T(2,128)S(1)}, f32[2,512]{1,0:T(2,128)S(1)}, f32[2,512]{1,0:T(2,128)S(1)}) custom-call(s32[32]{0:T(128)S(1)} %get-tuple-element.8.table_ref, f32[2,512]{1,0:T(2,128)S(1)} %get-tuple-element.9.own_ref, bf16[512,1024]{1,0:T(8,128)(2,1)S(1)} %collective-permute-done.z_ref, ...), custom_call_target="tpu_custom_call" | custom-call | flops 1610612736 | bytes 5242880 | tf_op jit(solution)/shard_map/pallas_call | solution.py:204
  48.5 1.9 %collective-permute-start.4 = (f32[2,512]{1,0:T(2,128)S(1)}, f32[2,512]{1,0:T(2,128)S(1)}, u32[]{:S(2)}, u32[]{:S(2)}) collective-permute-start(f32[2,512]{1,0:T(2,128)S(1)} %get-tuple-element.11), channel_id=1, source_target_pairs={{0,3},{1,0},{2,1},{3,2},{4,7},{5,4},{6,5},{7,6},{8,11},{9,8},{10,9... | collective-permute-start | bytes 12296 | tf_op jit(solution)/shard_map/ppermute | solution.py:248
  50.4 1.9 %collective-permute-start.5 = (f32[2,512]{1,0:T(2,128)S(1)}, f32[2,512]{1,0:T(2,128)S(1)}, u32[]{:S(2)}, u32[]{:S(2)}) collective-permute-start(f32[2,512]{1,0:T(2,128)S(1)} %get-tuple-element.12), channel_id=1, source_target_pairs={{0,5},{1,2},{2,3},{3,4},{4,9},{5,6},{6,7},{7,8},{8,13},{9,10},{10,... | collective-permute-start | bytes 12296 | tf_op jit(solution)/shard_map/ppermute | solution.py:247
  52.4 12.7 %collective-permute-start.6 = (f32[2,512]{1,0:T(2,128)S(1)}, f32[2,512]{1,0:T(2,128)S(1)}, u32[]{:S(2)}, u32[]{:S(2)}) collective-permute-start(f32[2,512]{1,0:T(2,128)S(1)} %get-tuple-element.13), channel_id=1, source_target_pairs={{4,0},{5,1},{6,2},{7,3},{8,4},{9,5},{10,6},{11,7},{12,8},{13,9},{1... | collective-permute-start | bytes 12296 | tf_op jit(solution)/shard_map/ppermute | solution.py:249
  65.0 0.0 collective-permute-done.4
  65.0 0.0 collective-permute-done.5
  65.0 1.3 %collective-permute-done.6 = f32[2,512]{1,0:T(2,128)S(1)} collective-permute-done((f32[2,512]{1,0:T(2,128)S(1)}, f32[2,512]{1,0:T(2,128)S(1)}, u32[]{:S(2)}, u32[]{:S(2)}) %collective-permute-start.6) | collective-permute-done | bytes 4128 | tf_op jit(solution)/shard_map/ppermute | solution.py:249
  66.3 0.6 slice_add_fusion
  (1 shorter events, 0.0 us)
Async XLA Ops:
  0.6 1.6 %copy-start.1 = (bf16[512,1024]{1,0:T(8,128)(2,1)S(1)}, bf16[512,1024]{1,0:T(8,128)(2,1)}, u32[]{:S(2)}) copy-start(bf16[512,1024]{1,0:T(8,128)(2,1)} %param.2) | copy-start | bytes 3145732
  2.2 23.9 %copy-start = (s32[170]{0:T(256)S(1)}, s32[170]{0:T(256)}, u32[]{:S(2)}) copy-start(s32[170]{0:T(256)} %sizes_ref.1) | copy-start | bytes 2044
  2.5 33.6 %collective-permute-start = (bf16[512,1024]{1,0:T(8,128)(2,1)S(1)}, bf16[512,1024]{1,0:T(8,128)(2,1)S(1)}, u32[]{:S(2)}, u32[]{:S(2)}) collective-permute-start(bf16[512,1024]{1,0:T(8,128)(2,1)S(1)} %fusion.1.x_ref), channel_id=1, source_target_pairs={{0,4},{1,5},{2,6},{3,7},{4,8},{5,9},{6,10},{7,11},{8,12},{9,13},{1... | collective-permute-start | bytes 3145736 | tf_op jit(solution)/shard_map/ppermute | solution.py:240
  6.3 29.8 %collective-permute-start.1 = (bf16[512,1024]{1,0:T(8,128)(2,1)S(1)}, bf16[512,1024]{1,0:T(8,128)(2,1)S(1)}, u32[]{:S(2)}, u32[]{:S(2)}) collective-permute-start(bf16[512,1024]{1,0:T(8,128)(2,1)S(1)} %fusion.1.x_ref), channel_id=1, source_target_pairs={{3,0},{0,1},{1,2},{2,3},{7,4},{4,5},{5,6},{6,7},{11,8},{8,9},{9,10... | collective-permute-start | bytes 3145736 | tf_op jit(solution)/shard_map/ppermute | solution.py:241
  9.7 26.4 %collective-permute-start.2 = (bf16[512,1024]{1,0:T(8,128)(2,1)S(1)}, bf16[512,1024]{1,0:T(8,128)(2,1)}, u32[]{:S(2)}, u32[]{:S(2)}) collective-permute-start(bf16[512,1024]{1,0:T(8,128)(2,1)S(1)} %fusion.1.x_ref), channel_id=1, source_target_pairs={{5,0},{2,1},{3,2},{4,3},{9,4},{6,5},{7,6},{8,7},{13,8},{10,9},{11,... | collective-permute-start | bytes 3145736 | tf_op jit(solution)/shard_map/ppermute | solution.py:242
  11.0 36.8 %collective-permute-start.3 = (bf16[512,1024]{1,0:T(8,128)(2,1)S(1)}, bf16[512,1024]{1,0:T(8,128)(2,1)}, u32[]{:S(2)}, u32[]{:S(2)}) collective-permute-start(bf16[512,1024]{1,0:T(8,128)(2,1)S(1)} %fusion.1.x_ref), channel_id=1, source_target_pairs={{65,60},{64,63},{129,124},{128,127},{193,188},{192,191},{257,252},... | collective-permute-start | bytes 3145736 | tf_op jit(solution)/shard_map/ppermute | solution.py:243
  48.5 16.5 %collective-permute-start.4 = (f32[2,512]{1,0:T(2,128)S(1)}, f32[2,512]{1,0:T(2,128)S(1)}, u32[]{:S(2)}, u32[]{:S(2)}) collective-permute-start(f32[2,512]{1,0:T(2,128)S(1)} %get-tuple-element.11), channel_id=1, source_target_pairs={{0,3},{1,0},{2,1},{3,2},{4,7},{5,4},{6,5},{7,6},{8,11},{9,8},{10,9... | collective-permute-start | bytes 12296 | tf_op jit(solution)/shard_map/ppermute | solution.py:248
  50.4 14.6 %collective-permute-start.5 = (f32[2,512]{1,0:T(2,128)S(1)}, f32[2,512]{1,0:T(2,128)S(1)}, u32[]{:S(2)}, u32[]{:S(2)}) collective-permute-start(f32[2,512]{1,0:T(2,128)S(1)} %get-tuple-element.12), channel_id=1, source_target_pairs={{0,5},{1,2},{2,3},{3,4},{4,9},{5,6},{6,7},{7,8},{8,13},{9,10},{10,... | collective-permute-start | bytes 12296 | tf_op jit(solution)/shard_map/ppermute | solution.py:247
  52.4 14.0 %collective-permute-start.6 = (f32[2,512]{1,0:T(2,128)S(1)}, f32[2,512]{1,0:T(2,128)S(1)}, u32[]{:S(2)}, u32[]{:S(2)}) collective-permute-start(f32[2,512]{1,0:T(2,128)S(1)} %get-tuple-element.13), channel_id=1, source_target_pairs={{4,0},{5,1},{6,2},{7,3},{8,4},{9,5},{10,6},{11,7},{12,8},{13,9},{1... | collective-permute-start | bytes 12296 | tf_op jit(solution)/shard_map/ppermute | solution.py:249

commit v3 on v2

v3 whole, which is shorter than its diff:
```python
import functools
import math

import jax
import jax.numpy as jnp
from jax import lax
from jax.experimental import pallas as pl
from jax.experimental.pallas import tpu as pltpu
from jax.sharding import PartitionSpec as P

MOST = 5
AXES = ("clus", "blk")
RING = 4

epsilon = 1e-06
threshold = 0.5
sharpness = 20.0
floor_value = -2.0

SLOTS = 3
OWN, UP, THIRD = range(SLOTS)
USED, SEGMENT = 8, 16
TABLE = 2 * SEGMENT
LANES = 128
TILE = 256


def upper_source(p):
    return p - 1 if p % RING else p + RING - 1


def lower_source(p):
    return p + 1 if p % RING else p + RING + 1


def routes(total):
    below, up, down = [], [], []
    for p in range(total):
        if p >= RING:
            below.append((p - RING, p))
        up.append((upper_source(p), p))
        if lower_source(p) < total:
            down.append((lower_source(p), p))
    return below, up, down


def inverse(route):
    return [(b, a) for a, b in route]


def unitize(values):
    widened = values.astype(jnp.float32)
    factor = lax.rsqrt(jnp.mean(widened * widened, axis=-1, keepdims=True) + epsilon) * (
        1.0 / math.sqrt(values.shape[-1])
    )
    return (widened * factor).astype(jnp.bfloat16)


def closeness_of(scores):
    return jax.nn.sigmoid(sharpness * (scores - threshold))


def score_block(rows, cols):
    return lax.dot_general(rows, cols, (((1,), (1,)), ((), ())), preferred_element_type=jnp.float32)


def fold_lanes(part, op):
    folded = part[:, :LANES]
    for k in range(1, part.shape[1] // LANES):
        folded = op(folded, part[:, k * LANES : (k + 1) * LANES])
    return folded


def fold_sublanes(part, reduce):
    return reduce(part.reshape(part.shape[0] // 8, 8, part.shape[1]), axis=0)


def write_table(total, sizes_ref, place_ref, table_ref):
    p = place_ref[0]
    x = lax.rem(p, RING)
    qu = jnp.where(x == 0, p + RING - 1, p - 1)
    qd = jnp.where(x == 0, p + RING + 1, p + 1)
    qz = p - RING

    def step(k, carry):
        end, at_p, at_u, at_d, at_z = carry
        end = end + sizes_ref[k]
        one = jnp.int32(1)
        zero = jnp.int32(0)
        return (
            end,
            at_p + jnp.where(end <= p, one, zero),
            at_u + jnp.where(end <= qu, one, zero),
            at_d + jnp.where(end <= qd, one, zero),
            at_z + jnp.where(end <= qz, one, zero),
        )

    nought = jnp.int32(0)
    _, mine, cu, cd, cz = lax.fori_loop(0, sizes_ref.shape[0], step, (nought,) * 5)
    has_d = qd < total
    has_z = qz >= 0
    parts = [
        [
            (cu == mine, OWN, UP),
            ((cz == mine) & has_z, THIRD, OWN),
            ((cz == cu) & has_z & (x > 0), THIRD, UP),
        ],
        [
            ((cd == mine) & has_d & (x == RING - 1), OWN, THIRD),
            ((cu == cd) & has_d, UP, THIRD),
        ],
    ]
    for part, wanted in enumerate(parts):
        base = part * SEGMENT
        n = nought
        used = [nought] * SLOTS
        for flag, i, j in wanted:
            table_ref[base + 1 + 2 * n] = jnp.int32(i)
            table_ref[base + 2 + 2 * n] = jnp.int32(j)
            bit = jnp.where(flag, jnp.int32(1), nought)
            used[i] = jnp.maximum(used[i], bit)
            used[j] = jnp.maximum(used[j], bit)
            n = n + bit
        table_ref[base] = n
        for slot in range(SLOTS):
            table_ref[base + USED + slot] = used[slot]


def diag_kernel(total, sizes_ref, place_ref, x_ref, out_ref, table_ref):
    rows = x_ref.shape[0]
    for c in range(rows // TILE):
        span = slice(c * TILE, (c + 1) * TILE)
        scores = score_block(x_ref[...], x_ref[span, :])
        self_pair = lax.broadcasted_iota(jnp.int32, scores.shape, 0) == (
            lax.broadcasted_iota(jnp.int32, scores.shape, 1) + c * TILE
        )
        near = jnp.where(self_pair, 0.0, closeness_of(scores))
        high = jnp.where(self_pair, floor_value, scores)
        out_ref[0:1, span] = jnp.max(high, axis=0, keepdims=True)
        out_ref[1:2, span] = jnp.sum(near, axis=0, keepdims=True)
    write_table(total, sizes_ref, place_ref, table_ref)


def pair_kernel(base, table_ref, *refs):
    *held, third_ref, up_ref, own_ref, out_own, out_up, out_third, slabs, best, count, sems = refs
    rows = slabs.shape[1]
    sources = [(OWN, own_ref), (UP, up_ref), (THIRD, third_ref)]
    for slot, ref in sources:

        @pl.when(table_ref[base + USED + slot] == 1)
        def _():
            pltpu.make_async_copy(ref, slabs.at[slot], sems.at[slot]).start()

    best[...] = jnp.full(best.shape, floor_value, jnp.float32)
    count[...] = jnp.zeros(count.shape, jnp.float32)
    for slot, ref in sources:

        @pl.when(table_ref[base + USED + slot] == 1)
        def _():
            pltpu.make_async_copy(ref, slabs.at[slot], sems.at[slot]).wait()

    def one(k, carry):
        i, j = table_ref[base + 2 * k + 1], table_ref[base + 2 * k + 2]
        high_rows = near_rows = None
        for c in range(rows // TILE):
            span = slice(c * TILE, (c + 1) * TILE)
            scores = score_block(slabs[i], slabs[j, span, :])
            near = closeness_of(scores)
            best[j, :, span] = jnp.maximum(best[j, :, span], fold_sublanes(scores, jnp.max))
            count[j, :, span] = count[j, :, span] + fold_sublanes(near, jnp.sum)
            high_part, near_part = fold_lanes(scores, jnp.maximum), fold_lanes(near, jnp.add)
            high_rows = high_part if high_rows is None else jnp.maximum(high_rows, high_part)
            near_rows = near_part if near_rows is None else near_rows + near_part
        best[i] = jnp.maximum(best[i], fold_sublanes(high_rows.T, jnp.max))
        count[i] = count[i] + fold_sublanes(near_rows.T, jnp.sum)
        return carry

    lax.fori_loop(0, table_ref[base], one, 0)

    for slot, ref in enumerate((out_own, out_up, out_third)):
        high = jnp.max(best[slot], axis=0, keepdims=True)
        near = jnp.sum(count[slot], axis=0, keepdims=True)
        if slot < len(held):
            high = jnp.maximum(held[slot][0:1, :], high)
            near = held[slot][1:2, :] + near
        ref[0:1, :] = high
        ref[1:2, :] = near


VMEM = pl.BlockSpec(memory_space=pltpu.VMEM)
SMEM = pl.BlockSpec(memory_space=pltpu.SMEM)
ANY = pl.BlockSpec(memory_space=pl.ANY)


def pair_stats(part, table, held, third, up, own_slab):
    rows, width = own_slab.shape
    stat = jax.ShapeDtypeStruct((2, rows), jnp.float32)
    return pl.pallas_call(
        functools.partial(pair_kernel, part * SEGMENT),
        in_specs=[SMEM] + [VMEM] * len(held) + [ANY] * 3,
        out_specs=[VMEM] * 3,
        out_shape=[stat] * 3,
        scratch_shapes=[
            pltpu.VMEM((SLOTS, rows, width), jnp.bfloat16),
            pltpu.VMEM((SLOTS, 8, rows), jnp.float32),
            pltpu.VMEM((SLOTS, 8, rows), jnp.float32),
            pltpu.SemaphoreType.DMA((SLOTS,)),
        ],
        compiler_params=pltpu.CompilerParams(vmem_limit_bytes=20 * 1024 * 1024),
        cost_estimate=pl.CostEstimate(flops=2 * 2 * rows * rows * width, bytes_accessed=3 * rows * width * 2, transcendentals=0),
    )(table, *held, third, up, own_slab)


def diag_stats(total, cluster_sizes, place, own_slab):
    rows, width = own_slab.shape
    return pl.pallas_call(
        functools.partial(diag_kernel, total),
        in_specs=[SMEM, SMEM, VMEM],
        out_specs=[VMEM, SMEM],
        out_shape=[
            jax.ShapeDtypeStruct((2, rows), jnp.float32),
            jax.ShapeDtypeStruct((TABLE,), jnp.int32),
        ],
        compiler_params=pltpu.CompilerParams(vmem_limit_bytes=16 * 1024 * 1024),
        cost_estimate=pl.CostEstimate(flops=2 * rows * rows * width, bytes_accessed=rows * width * 2, transcendentals=0),
    )(cluster_sizes, place, own_slab)


def shards(total):
    below_route, up_route, down_route = routes(total)

    def body(embeddings, cluster_sizes):
        normed = unitize(embeddings)
        below = lax.ppermute(normed, AXES, below_route)
        up = lax.ppermute(normed, AXES, up_route)
        down = lax.ppermute(normed, AXES, down_route)
        p = lax.axis_index(AXES)
        own, table = diag_stats(total, cluster_sizes, p[None].astype(jnp.int32), normed)
        own, for_up, for_below = pair_stats(0, table, [own], below, up, normed)
        mine, for_up, for_down = pair_stats(1, table, [own, for_up], down, up, normed)
        from_below = lax.ppermute(for_below, AXES, inverse(below_route))
        from_down = lax.ppermute(for_down, AXES, inverse(down_route))
        from_up = lax.ppermute(for_up, AXES, inverse(up_route))
        got_down = p >= 2
        got_below = p < total - RING
        best = jnp.maximum(mine[0], from_up[0])
        best = jnp.maximum(best, jnp.where(got_down, from_down[0], floor_value))
        best = jnp.maximum(best, jnp.where(got_below, from_below[0], floor_value))
        return best, mine[1] + from_up[1] + from_down[1] + from_below[1]

    return body


def solution(mesh):
    total = mesh.shape["blk"] * mesh.shape["clus"]
    return jax.shard_map(
        shards(total),
        mesh=mesh,
        in_specs=(P(AXES, None), P()),
        out_specs=(P(AXES), P(AXES)),
        check_vma=False,
    )
```

time: 67.2 us -> 58 us (0.86)
  the two profiles are of different devices: /device:TPU:16 before, /device:TPU:9 now
where the time goes in v3:
time: 58 us; the launch traced here: 57.7 us
  starting transfers between devices  32.4 us (56%)
  waiting for transfers between devices  15.2 us (26%)
  Pallas kernels  6.86 us (12%)
  other arithmetic  2.43 us (4%)
  between operations  0.77 us (1%)
    ppermute x1, waiting for transfers between devices, body(): below = lax.ppermute(normed, AXES, below_route)  12 us
    ppermute x1, starting transfers between devices, body(): down = lax.ppermute(normed, AXES, down_route)  11.5 us
    ppermute x1, starting transfers between devices, body(): from_below = lax.ppermute(for_below, AXES, inverse(below_route))  9.2 us
    pallas_call x1, Pallas kernels, diag_stats(): pl.pallas_call(functools.partial(diag_kernel, total), in_specs=[SMEM, SME...  4.43 us
    ppermute x1, starting transfers between devices, body(): below = lax.ppermute(normed, AXES, below_route)  3.55 us
    ppermute x1, waiting for transfers between devices, body(): from_down = lax.ppermute(for_down, AXES, inverse(down_route))  3.19 us
    ppermute x1, starting transfers between devices, body(): up = lax.ppermute(normed, AXES, up_route)  3.12 us
    ppermute x1, starting transfers between devices, body(): from_up = lax.ppermute(for_up, AXES, inverse(up_route))  3.11 us
  transfers between devices with their start and end apart: 6, of which 2 were waited for; matrix products, arithmetic and copies ran while one was open for 0% of the time, Pallas kernels for 12%

profile of v3, /device:TPU:9, one launch (start us, length us, event | category | flops | bytes accessed | tf_op | source)
XLA Modules:
  0.0 57.7 jit_solution(15269103013641335492)
XLA Ops:
  0.6 0.0 copy-start.1
  0.6 1.6 %fusion = f32[512]{0:T(512)S(1)} fusion(bf16[512,1024]{1,0:T(8,128)(2,1)} %param.2), kind=kLoop, calls=%fused_computation.2 | loop fusion | flops 1572352 | bytes 1050624 | tf_op jit(solution)/shard_map/reduce_sum | solution.py:53
  2.2 0.0 copy-done.1
  2.2 0.0 copy-start
  2.3 0.2 fusion.1.x_ref.refs_3_.refs_4_
  2.5 3.5 %collective-permute-start = (bf16[512,1024]{1,0:T(8,128)(2,1)S(1)}, bf16[512,1024]{1,0:T(8,128)(2,1)}, u32[]{:S(2)}, u32[]{:S(2)}) collective-permute-start(bf16[512,1024]{1,0:T(8,128)(2,1)S(1)} %fusion.1.x_ref.refs_3_.refs_4_), channel_id=1, source_target_pairs={{0,4},{1,5},{2,6},{3,7},{4,8},{5,9},{6,10},{7,11},{8,12},{9,13},{1... | collective-permute-start | bytes 3145736 | tf_op jit(solution)/shard_map/ppermute | solution.py:234
  6.1 3.1 %collective-permute-start.1 = (bf16[512,1024]{1,0:T(8,128)(2,1)S(1)}, bf16[512,1024]{1,0:T(8,128)(2,1)S(1)}, u32[]{:S(2)}, u32[]{:S(2)}) collective-permute-start(bf16[512,1024]{1,0:T(8,128)(2,1)S(1)} %fusion.1.x_ref.refs_3_.refs_4_), channel_id=1, source_target_pairs={{3,0},{0,1},{1,2},{2,3},{7,4},{4,5},{5,6},{6,7},{11,8},{8,9},{9,10... | collective-permute-start | bytes 3145736 | tf_op jit(solution)/shard_map/ppermute | solution.py:235
  9.2 11.5 %collective-permute-start.2 = (bf16[512,1024]{1,0:T(8,128)(2,1)S(1)}, bf16[512,1024]{1,0:T(8,128)(2,1)S(1)}, u32[]{:S(2)}, u32[]{:S(2)}) collective-permute-start(bf16[512,1024]{1,0:T(8,128)(2,1)S(1)} %fusion.1.x_ref.refs_3_.refs_4_), channel_id=1, source_target_pairs={{5,0},{2,1},{3,2},{4,3},{9,4},{6,5},{7,6},{8,7},{13,8},{10,9},{11,... | collective-permute-start | bytes 3145736 | tf_op jit(solution)/shard_map/ppermute | solution.py:236
  20.7 0.0 copy-done
  20.7 4.4 %shard_map.41 = (f32[2,512]{1,0:T(2,128)S(1)}, s32[32]{0:T(128)S(1)}) custom-call(s32[170]{0:T(256)S(1)} %copy-done, s32[1]{0:T(128)} %bitcast.place_ref, bf16[512,1024]{1,0:T(8,128)(2,1)S(1)} %fusion.1.x_ref.refs_3_.refs_4_), custom_call_target="tpu_custom_call" | custom-call | flops 536870912 | bytes 1048576 | tf_op jit(solution)/shard_map/pallas_call | solution.py:216
  25.2 12.0 %collective-permute-done.refs_1_ = bf16[512,1024]{1,0:T(8,128)(2,1)} collective-permute-done((bf16[512,1024]{1,0:T(8,128)(2,1)S(1)}, bf16[512,1024]{1,0:T(8,128)(2,1)}, u32[]{:S(2)}, u32[]{:S(2)}) %collective-permute-start) | collective-permute-done | bytes 1048608 | tf_op jit(solution)/shard_map/ppermute | solution.py:234
  37.2 0.0 collective-permute-done.1.refs_2_.refs_3_
  37.2 0.6 %shard_map.42 = (f32[2,512]{1,0:T(2,128)S(1)}, f32[2,512]{1,0:T(2,128)S(1)}, f32[2,512]{1,0:T(2,128)S(1)}) custom-call(s32[32]{0:T(128)S(1)} %get-tuple-element.10.table_ref, f32[2,512]{1,0:T(2,128)S(1)} %get-tuple-element.11.refs_0_, bf16[512,1024]{1,0:T(8,128)(2,1)} %collective-permute-done.refs_1_, ...), custom_call_target="tpu_custom_call" | custom-call | flops 1073741824 | bytes 3145728 | tf_op jit(solution)/shard_map/pallas_call | solution.py:198
  37.8 9.2 %collective-permute-start.5 = (f32[2,512]{1,0:T(2,128)S(1)}, f32[2,512]{1,0:T(2,128)S(1)}, u32[]{:S(2)}, u32[]{:S(2)}) collective-permute-start(f32[2,512]{1,0:T(2,128)S(1)} %get-tuple-element.17), channel_id=1, source_target_pairs={{4,0},{5,1},{6,2},{7,3},{8,4},{9,5},{10,6},{11,7},{12,8},{13,9},{1... | collective-permute-start | bytes 12296 | tf_op jit(solution)/shard_map/ppermute | solution.py:241
  47.0 0.0 collective-permute-done.2.refs_2_
  47.1 1.8 %shard_map.43 = (f32[2,512]{1,0:T(2,128)S(1)}, f32[2,512]{1,0:T(2,128)S(1)}, f32[2,512]{1,0:T(2,128)S(1)}) custom-call(s32[32]{0:T(128)S(1)} %get-tuple-element.10.table_ref, f32[2,512]{1,0:T(2,128)S(1)} %get-tuple-element.12.refs_0_, f32[2,512]{1,0:T(2,128)S(1)} %get-tuple-element.13.refs_1_, bf16[512,1024]{1,0:T(8,128)(2,1)S(1)} %collective-permute-done.2.refs_2_, ...), custom_call_target="tpu_custom_call" | custom-call | flops 1073741824 | bytes 3145728 | tf_op jit(solution)/shard_map/pallas_call | solution.py:198
  48.9 1.9 %collective-permute-start.4 = (f32[2,512]{1,0:T(2,128)S(1)}, f32[2,512]{1,0:T(2,128)S(1)}, u32[]{:S(2)}, u32[]{:S(2)}) collective-permute-start(f32[2,512]{1,0:T(2,128)S(1)} %get-tuple-element.16), channel_id=1, source_target_pairs={{0,5},{1,2},{2,3},{3,4},{4,9},{5,6},{6,7},{7,8},{8,13},{9,10},{10,... | collective-permute-start | bytes 12296 | tf_op jit(solution)/shard_map/ppermute | solution.py:242
  50.8 3.1 %collective-permute-start.3 = (f32[2,512]{1,0:T(2,128)S(1)}, f32[2,512]{1,0:T(2,128)S(1)}, u32[]{:S(2)}, u32[]{:S(2)}) collective-permute-start(f32[2,512]{1,0:T(2,128)S(1)} %get-tuple-element.15), channel_id=1, source_target_pairs={{0,3},{1,0},{2,1},{3,2},{4,7},{5,4},{6,5},{7,6},{8,11},{9,8},{10,9... | collective-permute-start | bytes 12296 | tf_op jit(solution)/shard_map/ppermute | solution.py:243
  53.9 0.0 collective-permute-done.5
  53.9 3.2 %collective-permute-done.4 = f32[2,512]{1,0:T(2,128)S(1)} collective-permute-done((f32[2,512]{1,0:T(2,128)S(1)}, f32[2,512]{1,0:T(2,128)S(1)}, u32[]{:S(2)}, u32[]{:S(2)}) %collective-permute-start.4) | collective-permute-done | bytes 4128 | tf_op jit(solution)/shard_map/ppermute | solution.py:242
  57.1 0.0 collective-permute-done.3
  57.1 0.6 %slice_add_fusion = (f32[1,512]{1,0:T(1,128)}, f32[1,512]{1,0:T(1,128)}) fusion(f32[2,512]{1,0:T(2,128)S(1)} %collective-permute-done.5, f32[2,512]{1,0:T(2,128)S(1)} %collective-permute-done.4, f32[2,512]{1,0:T(2,128)S(1)} %collective-permute-done.3, f32[2,512]{1,0:T(2,128)S(1)} %get-tuple-element.14, pred[]{:T(512)S(6)} %lt.3, pred[]{:T(512)S(6)} %ge.3), kind=kLoop, calls=%fused_computation.8 | loop fusion | flops 4096 | bytes 20482 | tf_op jit(solution)/shard_map/add | solution.py:249
  (1 shorter events, 0.0 us)
Async XLA Ops:
  0.6 1.6 %copy-start.1 = (bf16[512,1024]{1,0:T(8,128)(2,1)S(1)}, bf16[512,1024]{1,0:T(8,128)(2,1)}, u32[]{:S(2)}) copy-start(bf16[512,1024]{1,0:T(8,128)(2,1)} %param.2) | copy-start | bytes 3145732
  2.2 18.5 %copy-start = (s32[170]{0:T(256)S(1)}, s32[170]{0:T(256)}, u32[]{:S(2)}) copy-start(s32[170]{0:T(256)} %sizes_ref.1) | copy-start | bytes 2044
  2.5 34.7 %collective-permute-start = (bf16[512,1024]{1,0:T(8,128)(2,1)S(1)}, bf16[512,1024]{1,0:T(8,128)(2,1)}, u32[]{:S(2)}, u32[]{:S(2)}) collective-permute-start(bf16[512,1024]{1,0:T(8,128)(2,1)S(1)} %fusion.1.x_ref.refs_3_.refs_4_), channel_id=1, source_target_pairs={{0,4},{1,5},{2,6},{3,7},{4,8},{5,9},{6,10},{7,11},{8,12},{9,13},{1... | collective-permute-start | bytes 3145736 | tf_op jit(solution)/shard_map/ppermute | solution.py:234
  6.1 31.1 %collective-permute-start.1 = (bf16[512,1024]{1,0:T(8,128)(2,1)S(1)}, bf16[512,1024]{1,0:T(8,128)(2,1)S(1)}, u32[]{:S(2)}, u32[]{:S(2)}) collective-permute-start(bf16[512,1024]{1,0:T(8,128)(2,1)S(1)} %fusion.1.x_ref.refs_3_.refs_4_), channel_id=1, source_target_pairs={{3,0},{0,1},{1,2},{2,3},{7,4},{4,5},{5,6},{6,7},{11,8},{8,9},{9,10... | collective-permute-start | bytes 3145736 | tf_op jit(solution)/shard_map/ppermute | solution.py:235
  9.2 37.9 %collective-permute-start.2 = (bf16[512,1024]{1,0:T(8,128)(2,1)S(1)}, bf16[512,1024]{1,0:T(8,128)(2,1)S(1)}, u32[]{:S(2)}, u32[]{:S(2)}) collective-permute-start(bf16[512,1024]{1,0:T(8,128)(2,1)S(1)} %fusion.1.x_ref.refs_3_.refs_4_), channel_id=1, source_target_pairs={{5,0},{2,1},{3,2},{4,3},{9,4},{6,5},{7,6},{8,7},{13,8},{10,9},{11,... | collective-permute-start | bytes 3145736 | tf_op jit(solution)/shard_map/ppermute | solution.py:236
  37.8 16.1 %collective-permute-start.5 = (f32[2,512]{1,0:T(2,128)S(1)}, f32[2,512]{1,0:T(2,128)S(1)}, u32[]{:S(2)}, u32[]{:S(2)}) collective-permute-start(f32[2,512]{1,0:T(2,128)S(1)} %get-tuple-element.17), channel_id=1, source_target_pairs={{4,0},{5,1},{6,2},{7,3},{8,4},{9,5},{10,6},{11,7},{12,8},{13,9},{1... | collective-permute-start | bytes 12296 | tf_op jit(solution)/shard_map/ppermute | solution.py:241
  48.9 8.2 %collective-permute-start.4 = (f32[2,512]{1,0:T(2,128)S(1)}, f32[2,512]{1,0:T(2,128)S(1)}, u32[]{:S(2)}, u32[]{:S(2)}) collective-permute-start(f32[2,512]{1,0:T(2,128)S(1)} %get-tuple-element.16), channel_id=1, source_target_pairs={{0,5},{1,2},{2,3},{3,4},{4,9},{5,6},{6,7},{7,8},{8,13},{9,10},{10,... | collective-permute-start | bytes 12296 | tf_op jit(solution)/shard_map/ppermute | solution.py:242
  50.8 6.3 %collective-permute-start.3 = (f32[2,512]{1,0:T(2,128)S(1)}, f32[2,512]{1,0:T(2,128)S(1)}, u32[]{:S(2)}, u32[]{:S(2)}) collective-permute-start(f32[2,512]{1,0:T(2,128)S(1)} %get-tuple-element.15), channel_id=1, source_target_pairs={{0,3},{1,0},{2,1},{3,2},{4,7},{5,4},{6,5},{7,6},{8,11},{9,8},{10,9... | collective-permute-start | bytes 12296 | tf_op jit(solution)/shard_map/ppermute | solution.py:243

commit v4 on v3

--- a/solution.py
+++ b/solution.py
@@ -17,12 +17,12 @@
 sharpness = 20.0
 floor_value = -2.0
 
-SLOTS = 3
-OWN, UP, THIRD = range(SLOTS)
-USED, SEGMENT = 8, 16
-TABLE = 2 * SEGMENT
+OWN, UP, DOWN, BELOW = range(4)
+BELOW_OWN, BELOW_UP, OWN_UP, OWN_UP_LATE, OWN_DOWN, UP_DOWN = range(6)
+TABLE = 8
 LANES = 128
 TILE = 256
+CHUNKS = 4
 
 
 def upper_source(p):
@@ -99,31 +99,18 @@
     _, mine, cu, cd, cz = lax.fori_loop(0, sizes_ref.shape[0], step, (nought,) * 5)
     has_d = qd < total
     has_z = qz >= 0
-    parts = [
-        [
-            (cu == mine, OWN, UP),
-            ((cz == mine) & has_z, THIRD, OWN),
-            ((cz == cu) & has_z & (x > 0), THIRD, UP),
-        ],
-        [
-            ((cd == mine) & has_d & (x == RING - 1), OWN, THIRD),
-            ((cu == cd) & has_d, UP, THIRD),
-        ],
-    ]
-    for part, wanted in enumerate(parts):
-        base = part * SEGMENT
-        n = nought
-        used = [nought] * SLOTS
-        for flag, i, j in wanted:
-            table_ref[base + 1 + 2 * n] = jnp.int32(i)
-            table_ref[base + 2 + 2 * n] = jnp.int32(j)
-            bit = jnp.where(flag, jnp.int32(1), nought)
-            used[i] = jnp.maximum(used[i], bit)
-            used[j] = jnp.maximum(used[j], bit)
-            n = n + bit
-        table_ref[base] = n
-        for slot in range(SLOTS):
-            table_ref[base + USED + slot] = used[slot]
+    with_up = cu == mine
+    below_up = (cz == cu) & has_z & (x > 0)
+    flags = {
+        BELOW_OWN: (cz == mine) & has_z,
+        BELOW_UP: below_up,
+        OWN_UP: with_up & ~below_up,
+        OWN_UP_LATE: with_up & below_up,
+        OWN_DOWN: (cd == mine) & has_d & (x == RING - 1),
+        UP_DOWN: (cu == cd) & has_d,
+    }
+    for place, flag in flags.items():
+        table_ref[place] = jnp.where(flag, jnp.int32(1), nought)
 
 
 def diag_kernel(total, sizes_ref, place_ref, x_ref, out_ref, table_ref):
@@ -141,50 +128,57 @@
     write_table(total, sizes_ref, place_ref, table_ref)
 
 
-def pair_kernel(base, table_ref, *refs):
-    *held, third_ref, up_ref, own_ref, out_own, out_up, out_third, slabs, best, count, sems = refs
-    rows = slabs.shape[1]
-    sources = [(OWN, own_ref), (UP, up_ref), (THIRD, third_ref)]
-    for slot, ref in sources:
-
-        @pl.when(table_ref[base + USED + slot] == 1)
-        def _():
-            pltpu.make_async_copy(ref, slabs.at[slot], sems.at[slot]).start()
-
+def pair_kernel(slots, given, pairs, table_ref, *refs):
+    n = len(slots)
+    held = dict(zip(given, refs))
+    slab = dict(zip(slots, refs[len(given) :]))
+    out = dict(zip(slots, refs[len(given) + n :]))
+    best, count = refs[len(given) + 2 * n :]
+    at = {slot: k for k, slot in enumerate(slots)}
+    rows = best.shape[2]
     best[...] = jnp.full(best.shape, floor_value, jnp.float32)
     count[...] = jnp.zeros(count.shape, jnp.float32)
-    for slot, ref in sources:
-
-        @pl.when(table_ref[base + USED + slot] == 1)
-        def _():
-            pltpu.make_async_copy(ref, slabs.at[slot], sems.at[slot]).wait()
-
-    def one(k, carry):
-        i, j = table_ref[base + 2 * k + 1], table_ref[base + 2 * k + 2]
+
+    def score_pair(i, j):
         high_rows = near_rows = None
         for c in range(rows // TILE):
             span = slice(c * TILE, (c + 1) * TILE)
-            scores = score_block(slabs[i], slabs[j, span, :])
+            scores = score_block(slab[i][...], slab[j][span, :])
             near = closeness_of(scores)
-            best[j, :, span] = jnp.maximum(best[j, :, span], fold_sublanes(scores, jnp.max))
-            count[j, :, span] = count[j, :, span] + fold_sublanes(near, jnp.sum)
+            best[at[j], :, span] = jnp.maximum(best[at[j], :, span], fold_sublanes(scores, jnp.max))
+            count[at[j], :, span] = count[at[j], :, span] + fold_sublanes(near, jnp.sum)
             high_part, near_part = fold_lanes(scores, jnp.maximum), fold_lanes(near, jnp.add)
             high_rows = high_part if high_rows is None else jnp.maximum(high_rows, high_part)
             near_rows = near_part if near_rows is None else near_rows + near_part
-        best[i] = jnp.maximum(best[i], fold_sublanes(high_rows.T, jnp.max))
-        count[i] = count[i] + fold_sublanes(near_rows.T, jnp.sum)
-        return carry
-
-    lax.fori_loop(0, table_ref[base], one, 0)
-
-    for slot, ref in enumerate((out_own, out_up, out_third)):
-        high = jnp.max(best[slot], axis=0, keepdims=True)
-        near = jnp.sum(count[slot], axis=0, keepdims=True)
-        if slot < len(held):
+        best[at[i]] = jnp.maximum(best[at[i]], fold_sublanes(high_rows.T, jnp.max))
+        count[at[i]] = count[at[i]] + fold_sublanes(near_rows.T, jnp.sum)
+
+    for flag, i, j in pairs:
+        pl.when(table_ref[flag] == 1)(functools.partial(score_pair, i, j))
+
+    for slot in slots:
+        high = jnp.max(best[at[slot]], axis=0, keepdims=True)
+        near = jnp.sum(count[at[slot]], axis=0, keepdims=True)
+        if slot in held:
             high = jnp.maximum(held[slot][0:1, :], high)
             near = held[slot][1:2, :] + near
-        ref[0:1, :] = high
-        ref[1:2, :] = near
+        out[slot][0:1, :] = high
+        out[slot][1:2, :] = near
+
+
+def normalise_kernel(x_ref, out_ref, raw, sems):
+    rows, width = raw.shape
+    step = rows // CHUNKS
+    spans = [slice(k * step, (k + 1) * step) for k in range(CHUNKS)]
+    copies = [pltpu.make_async_copy(x_ref.at[s, :], raw.at[s, :], sems.at[k]) for k, s in enumerate(spans)]
+    for copy in copies:
+        copy.start()
+    for copy, s in zip(copies, spans):
+        copy.wait()
+        widened = raw[s, :].astype(jnp.float32)
+        mean = jnp.sum(fold_lanes(widened * widened, jnp.add), axis=1, keepdims=True) * (1.0 / width)
+        factor = lax.rsqrt(mean + epsilon) * (1.0 / math.sqrt(width))
+        out_ref[s, :] = (widened * factor).astype(jnp.bfloat16)
 
 
 VMEM = pl.BlockSpec(memory_space=pltpu.VMEM)
@@ -192,23 +186,32 @@
 ANY = pl.BlockSpec(memory_space=pl.ANY)
 
 
-def pair_stats(part, table, held, third, up, own_slab):
-    rows, width = own_slab.shape
-    stat = jax.ShapeDtypeStruct((2, rows), jnp.float32)
+def pair_stats(table, stats, slabs, pairs):
+    slots, given = list(slabs), list(stats)
+    rows, width = slabs[OWN].shape
+    outs = pl.pallas_call(
+        functools.partial(pair_kernel, slots, given, pairs),
+        in_specs=[SMEM] + [VMEM] * (len(given) + len(slots)),
+        out_specs=[VMEM] * len(slots),
+        out_shape=[jax.ShapeDtypeStruct((2, rows), jnp.float32)] * len(slots),
+        scratch_shapes=[pltpu.VMEM((len(slots), 8, rows), jnp.float32)] * 2,
+        compiler_params=pltpu.CompilerParams(vmem_limit_bytes=20 * 1024 * 1024),
+        cost_estimate=pl.CostEstimate(flops=2 * rows * rows * width, bytes_accessed=len(slots) * rows * width * 2, transcendentals=0),
+    )(table, *[stats[s] for s in given], *[slabs[s] for s in slots])
+    return dict(zip(slots, outs))
+
+
+def normalised(embeddings):
+    rows, width = embeddings.shape
     return pl.pallas_call(
-        functools.partial(pair_kernel, part * SEGMENT),
-        in_specs=[SMEM] + [VMEM] * len(held) + [ANY] * 3,
-        out_specs=[VMEM] * 3,
-        out_shape=[stat] * 3,
-        scratch_shapes=[
-            pltpu.VMEM((SLOTS, rows, width), jnp.bfloat16),
-            pltpu.VMEM((SLOTS, 8, rows), jnp.float32),
-            pltpu.VMEM((SLOTS, 8, rows), jnp.float32),
-            pltpu.SemaphoreType.DMA((SLOTS,)),
-        ],
-        compiler_params=pltpu.CompilerParams(vmem_limit_bytes=20 * 1024 * 1024),
-        cost_estimate=pl.CostEstimate(flops=2 * 2 * rows * rows * width, bytes_accessed=3 * rows * width * 2, transcendentals=0),
-    )(table, *held, third, up, own_slab)
+        normalise_kernel,
+        in_specs=[ANY],
+        out_specs=VMEM,
+        out_shape=jax.ShapeDtypeStruct((rows, width), jnp.bfloat16),
+        scratch_shapes=[pltpu.VMEM((rows, width), jnp.bfloat16), pltpu.SemaphoreType.DMA((CHUNKS,))],
+        compiler_params=pltpu.CompilerParams(vmem_limit_bytes=16 * 1024 * 1024),
+        cost_estimate=pl.CostEstimate(flops=4 * rows * width, bytes_accessed=2 * rows * width * 2, transcendentals=rows),
+    )(embeddings)
 
 
 def diag_stats(total, cluster_sizes, place, own_slab):
@@ -236,8 +239,21 @@
         down = lax.ppermute(normed, AXES, down_route)
         p = lax.axis_index(AXES)
         own, table = diag_stats(total, cluster_sizes, p[None].astype(jnp.int32), normed)
-        own, for_up, for_below = pair_stats(0, table, [own], below, up, normed)
-        mine, for_up, for_down = pair_stats(1, table, [own, for_up], down, up, normed)
+        stats = pair_stats(table, {OWN: own}, {BELOW: below, OWN: normed}, [(BELOW_OWN, BELOW, OWN)])
+        stats = pair_stats(
+            table,
+            stats,
+            {BELOW: below, UP: up, OWN: normed},
+            [(BELOW_UP, BELOW, UP), (OWN_UP, OWN, UP)],
+        )
+        for_below = stats.pop(BELOW)
+        stats = pair_stats(
+            table,
+            stats,
+            {DOWN: down, UP: up, OWN: normed},
+            [(OWN_UP_LATE, OWN, UP), (OWN_DOWN, OWN, DOWN), (UP_DOWN, UP, DOWN)],
+        )
+        mine, for_up, for_down = stats[OWN], stats[UP], stats[DOWN]
         from_below = lax.ppermute(for_below, AXES, inverse(below_route))
         from_down = lax.ppermute(for_down, AXES, inverse(down_route))
         from_up = lax.ppermute(for_up, AXES, inverse(up_route))

time: 58 us -> 57 us (0.983)
  the two profiles are of different devices: /device:TPU:9 before, /device:TPU:1 now
where the time goes in v4:
time: 57 us; the launch traced here: 56.7 us
  starting transfers between devices  33.3 us (58%)
  waiting for transfers between devices  13.4 us (24%)
  Pallas kernels  6.79 us (12%)
  other arithmetic  2.43 us (4%)
  between operations  0.78 us (1%)
    ppermute x1, waiting for transfers between devices, body(): below = lax.ppermute(normed, AXES, below_route)  12.2 us
    ppermute x1, starting transfers between devices, body(): down = lax.ppermute(normed, AXES, down_route)  11.5 us
    ppermute x1, starting transfers between devices, body(): from_below = lax.ppermute(for_below, AXES, inverse(below_route))  7.23 us
    ppermute x1, starting transfers between devices, body(): from_up = lax.ppermute(for_up, AXES, inverse(up_route))  5.15 us
    ppermute x1, starting transfers between devices, body(): below = lax.ppermute(normed, AXES, below_route)  4.38 us
    pallas_call x1, Pallas kernels, diag_stats(): pl.pallas_call(functools.partial(diag_kernel, total), in_specs=[SMEM, SME...  4.33 us
    ppermute x1, starting transfers between devices, body(): up = lax.ppermute(normed, AXES, up_route)  3.12 us
    pallas_call x3, Pallas kernels, pair_stats(): pl.pallas_call(functools.partial(pair_kernel, slots, given, pairs), in_sp...  2.46 us
  transfers between devices with their start and end apart: 6, of which 2 were waited for; matrix products, arithmetic and copies ran while one was open for 0% of the time, Pallas kernels for 12%

profile of v4, /device:TPU:1, one launch (start us, length us, event | category | flops | bytes accessed | tf_op | source)
XLA Modules:
  0.0 56.7 jit_solution(15123262046665550842)
XLA Ops:
  0.6 0.0 copy-start.1
  0.6 1.6 %fusion = f32[512]{0:T(512)S(1)} fusion(bf16[512,1024]{1,0:T(8,128)(2,1)} %param.2), kind=kLoop, calls=%fused_computation.2 | loop fusion | flops 1572352 | bytes 1050624 | tf_op jit(solution)/shard_map/reduce_sum | solution.py:53
  2.2 0.0 copy-done.1
  2.2 0.0 copy-start
  2.3 0.2 fusion.1.x_ref.refs_2_.refs_4_
  2.5 4.4 %collective-permute-start = (bf16[512,1024]{1,0:T(8,128)(2,1)S(1)}, bf16[512,1024]{1,0:T(8,128)(2,1)S(1)}, u32[]{:S(2)}, u32[]{:S(2)}) collective-permute-start(bf16[512,1024]{1,0:T(8,128)(2,1)S(1)} %fusion.1.x_ref.refs_2_.refs_4_), channel_id=1, source_target_pairs={{0,4},{1,5},{2,6},{3,7},{4,8},{5,9},{6,10},{7,11},{8,12},{9,13},{1... | collective-permute-start | bytes 3145736 | tf_op jit(solution)/shard_map/ppermute | solution.py:237
  6.9 3.1 %collective-permute-start.1 = (bf16[512,1024]{1,0:T(8,128)(2,1)S(1)}, bf16[512,1024]{1,0:T(8,128)(2,1)S(1)}, u32[]{:S(2)}, u32[]{:S(2)}) collective-permute-start(bf16[512,1024]{1,0:T(8,128)(2,1)S(1)} %fusion.1.x_ref.refs_2_.refs_4_), channel_id=1, source_target_pairs={{3,0},{0,1},{1,2},{2,3},{7,4},{4,5},{5,6},{6,7},{11,8},{8,9},{9,10... | collective-permute-start | bytes 3145736 | tf_op jit(solution)/shard_map/ppermute | solution.py:238
  10.0 11.5 %collective-permute-start.2 = (bf16[512,1024]{1,0:T(8,128)(2,1)S(1)}, bf16[512,1024]{1,0:T(8,128)(2,1)}, u32[]{:S(2)}, u32[]{:S(2)}) collective-permute-start(bf16[512,1024]{1,0:T(8,128)(2,1)S(1)} %fusion.1.x_ref.refs_2_.refs_4_), channel_id=1, source_target_pairs={{5,0},{2,1},{3,2},{4,3},{9,4},{6,5},{7,6},{8,7},{13,8},{10,9},{11,... | collective-permute-start | bytes 3145736 | tf_op jit(solution)/shard_map/ppermute | solution.py:239
  21.6 0.0 copy-done
  21.6 4.3 %shard_map.41 = (f32[2,512]{1,0:T(2,128)S(1)}, s32[8]{0:T(128)S(1)}) custom-call(s32[170]{0:T(256)S(1)} %copy-done, s32[1]{0:T(128)} %bitcast.place_ref, bf16[512,1024]{1,0:T(8,128)(2,1)S(1)} %fusion.1.x_ref.refs_2_.refs_4_), custom_call_target="tpu_custom_call" | custom-call | flops 536870912 | bytes 1048576 | tf_op jit(solution)/shard_map/pallas_call | solution.py:219
  25.9 12.2 %collective-permute-done.refs_1_.refs_2_ = bf16[512,1024]{1,0:T(8,128)(2,1)S(1)} collective-permute-done((bf16[512,1024]{1,0:T(8,128)(2,1)S(1)}, bf16[512,1024]{1,0:T(8,128)(2,1)S(1)}, u32[]{:S(2)}, u32[]{:S(2)}) %collective-permute-start) | collective-permute-done | bytes 1048608 | tf_op jit(solution)/shard_map/ppermute | solution.py:237
  38.1 0.6 %shard_map.42 = (f32[2,512]{1,0:T(2,128)S(1)}, f32[2,512]{1,0:T(2,128)S(1)}) custom-call(s32[8]{0:T(128)S(1)} %get-tuple-element.12.table_ref, f32[2,512]{1,0:T(2,128)S(1)} %get-tuple-element.13.refs_0_, bf16[512,1024]{1,0:T(8,128)(2,1)S(1)} %collective-permute-done.refs_1_.refs_2_, bf16[512,1024]{1,0:T(8,128)(2,1)S(1)} %fusion.1.x_ref.refs_2_.refs_4_), custom_call_target="tpu_custom_call" | custom-call | flops 536870912 | bytes 2097152 | tf_op jit(solution)/shard_map/pallas_call | solution.py:192
  38.7 0.0 collective-permute-done.1.refs_3_
  38.7 0.6 %shard_map.43 = (f32[2,512]{1,0:T(2,128)S(1)}, f32[2,512]{1,0:T(2,128)S(1)}, f32[2,512]{1,0:T(2,128)S(1)}) custom-call(s32[8]{0:T(128)S(1)} %get-tuple-element.12.table_ref, f32[2,512]{1,0:T(2,128)S(1)} %get-tuple-element.14.refs_0_, f32[2,512]{1,0:T(2,128)S(1)} %get-tuple-element.15.refs_1_, bf16[512,1024]{1,0:T(8,128)(2,1)S(1)} %collective-permute-done.refs_1_.refs_2_, ...), custom_call_target="tpu_custom_call" | custom-call | flops 536870912 | bytes 3145728 | tf_op jit(solution)/shard_map/pallas_call | solution.py:192
  39.3 7.2 %collective-permute-start.5 = (f32[2,512]{1,0:T(2,128)S(1)}, f32[2,512]{1,0:T(2,128)S(1)}, u32[]{:S(2)}, u32[]{:S(2)}) collective-permute-start(f32[2,512]{1,0:T(2,128)S(1)} %get-tuple-element.21), channel_id=1, source_target_pairs={{4,0},{5,1},{6,2},{7,3},{8,4},{9,5},{10,6},{11,7},{12,8},{13,9},{1... | collective-permute-start | bytes 12296 | tf_op jit(solution)/shard_map/ppermute | solution.py:257
  46.5 0.0 collective-permute-done.2.refs_2_
  46.6 1.3 %shard_map.44 = (f32[2,512]{1,0:T(2,128)S(1)}, f32[2,512]{1,0:T(2,128)S(1)}, f32[2,512]{1,0:T(2,128)S(1)}) custom-call(s32[8]{0:T(128)S(1)} %get-tuple-element.12.table_ref, f32[2,512]{1,0:T(2,128)S(1)} %get-tuple-element.16.refs_0_, f32[2,512]{1,0:T(2,128)S(1)} %get-tuple-element.17.refs_1_, bf16[512,1024]{1,0:T(8,128)(2,1)} %collective-permute-done.2.refs_2_, ...), custom_call_target="tpu_custom_call" | custom-call | flops 536870912 | bytes 3145728 | tf_op jit(solution)/shard_map/pallas_call | solution.py:192
  47.9 1.9 %collective-permute-start.4 = (f32[2,512]{1,0:T(2,128)S(1)}, f32[2,512]{1,0:T(2,128)S(1)}, u32[]{:S(2)}, u32[]{:S(2)}) collective-permute-start(f32[2,512]{1,0:T(2,128)S(1)} %get-tuple-element.20), channel_id=1, source_target_pairs={{0,5},{1,2},{2,3},{3,4},{4,9},{5,6},{6,7},{7,8},{8,13},{9,10},{10,... | collective-permute-start | bytes 12296 | tf_op jit(solution)/shard_map/ppermute | solution.py:258
  49.8 5.2 %collective-permute-start.3 = (f32[2,512]{1,0:T(2,128)S(1)}, f32[2,512]{1,0:T(2,128)S(1)}, u32[]{:S(2)}, u32[]{:S(2)}) collective-permute-start(f32[2,512]{1,0:T(2,128)S(1)} %get-tuple-element.19), channel_id=1, source_target_pairs={{0,3},{1,0},{2,1},{3,2},{4,7},{5,4},{6,5},{7,6},{8,11},{9,8},{10,9... | collective-permute-start | bytes 12296 | tf_op jit(solution)/shard_map/ppermute | solution.py:259
  54.9 0.0 collective-permute-done.5
  55.0 1.1 %collective-permute-done.4 = f32[2,512]{1,0:T(2,128)S(1)} collective-permute-done((f32[2,512]{1,0:T(2,128)S(1)}, f32[2,512]{1,0:T(2,128)S(1)}, u32[]{:S(2)}, u32[]{:S(2)}) %collective-permute-start.4) | collective-permute-done | bytes 4128 | tf_op jit(solution)/shard_map/ppermute | solution.py:258
  56.1 0.0 collective-permute-done.3
  56.1 0.6 %slice_add_fusion = (f32[1,512]{1,0:T(1,128)}, f32[1,512]{1,0:T(1,128)}) fusion(f32[2,512]{1,0:T(2,128)S(1)} %collective-permute-done.5, f32[2,512]{1,0:T(2,128)S(1)} %collective-permute-done.4, f32[2,512]{1,0:T(2,128)S(1)} %collective-permute-done.3, f32[2,512]{1,0:T(2,128)S(1)} %get-tuple-element.18, pred[]{:T(512)S(6)} %lt.3, pred[]{:T(512)S(6)} %ge.3), kind=kLoop, calls=%fused_computation.8 | loop fusion | flops 4096 | bytes 20482 | tf_op jit(solution)/shard_map/add | solution.py:265
  (1 shorter events, 0.0 us)
Async XLA Ops:
  0.6 1.6 %copy-start.1 = (bf16[512,1024]{1,0:T(8,128)(2,1)S(1)}, bf16[512,1024]{1,0:T(8,128)(2,1)}, u32[]{:S(2)}) copy-start(bf16[512,1024]{1,0:T(8,128)(2,1)} %param.2) | copy-start | bytes 3145732
  2.2 19.3 %copy-start = (s32[170]{0:T(256)S(1)}, s32[170]{0:T(256)}, u32[]{:S(2)}) copy-start(s32[170]{0:T(256)} %sizes_ref.1) | copy-start | bytes 2044
  2.5 35.6 %collective-permute-start = (bf16[512,1024]{1,0:T(8,128)(2,1)S(1)}, bf16[512,1024]{1,0:T(8,128)(2,1)S(1)}, u32[]{:S(2)}, u32[]{:S(2)}) collective-permute-start(bf16[512,1024]{1,0:T(8,128)(2,1)S(1)} %fusion.1.x_ref.refs_2_.refs_4_), channel_id=1, source_target_pairs={{0,4},{1,5},{2,6},{3,7},{4,8},{5,9},{6,10},{7,11},{8,12},{9,13},{1... | collective-permute-start | bytes 3145736 | tf_op jit(solution)/shard_map/ppermute | solution.py:237
  6.9 31.8 %collective-permute-start.1 = (bf16[512,1024]{1,0:T(8,128)(2,1)S(1)}, bf16[512,1024]{1,0:T(8,128)(2,1)S(1)}, u32[]{:S(2)}, u32[]{:S(2)}) collective-permute-start(bf16[512,1024]{1,0:T(8,128)(2,1)S(1)} %fusion.1.x_ref.refs_2_.refs_4_), channel_id=1, source_target_pairs={{3,0},{0,1},{1,2},{2,3},{7,4},{4,5},{5,6},{6,7},{11,8},{8,9},{9,10... | collective-permute-start | bytes 3145736 | tf_op jit(solution)/shard_map/ppermute | solution.py:238
  10.0 36.5 %collective-permute-start.2 = (bf16[512,1024]{1,0:T(8,128)(2,1)S(1)}, bf16[512,1024]{1,0:T(8,128)(2,1)}, u32[]{:S(2)}, u32[]{:S(2)}) collective-permute-start(bf16[512,1024]{1,0:T(8,128)(2,1)S(1)} %fusion.1.x_ref.refs_2_.refs_4_), channel_id=1, source_target_pairs={{5,0},{2,1},{3,2},{4,3},{9,4},{6,5},{7,6},{8,7},{13,8},{10,9},{11,... | collective-permute-start | bytes 3145736 | tf_op jit(solution)/shard_map/ppermute | solution.py:239
  39.3 15.6 %collective-permute-start.5 = (f32[2,512]{1,0:T(2,128)S(1)}, f32[2,512]{1,0:T(2,128)S(1)}, u32[]{:S(2)}, u32[]{:S(2)}) collective-permute-start(f32[2,512]{1,0:T(2,128)S(1)} %get-tuple-element.21), channel_id=1, source_target_pairs={{4,0},{5,1},{6,2},{7,3},{8,4},{9,5},{10,6},{11,7},{12,8},{13,9},{1... | collective-permute-start | bytes 12296 | tf_op jit(solution)/shard_map/ppermute | solution.py:257
  47.9 8.2 %collective-permute-start.4 = (f32[2,512]{1,0:T(2,128)S(1)}, f32[2,512]{1,0:T(2,128)S(1)}, u32[]{:S(2)}, u32[]{:S(2)}) collective-permute-start(f32[2,512]{1,0:T(2,128)S(1)} %get-tuple-element.20), channel_id=1, source_target_pairs={{0,5},{1,2},{2,3},{3,4},{4,9},{5,6},{6,7},{7,8},{8,13},{9,10},{10,... | collective-permute-start | bytes 12296 | tf_op jit(solution)/shard_map/ppermute | solution.py:258
  49.8 6.3 %collective-permute-start.3 = (f32[2,512]{1,0:T(2,128)S(1)}, f32[2,512]{1,0:T(2,128)S(1)}, u32[]{:S(2)}, u32[]{:S(2)}) collective-permute-start(f32[2,512]{1,0:T(2,128)S(1)} %get-tuple-element.19), channel_id=1, source_target_pairs={{0,3},{1,0},{2,1},{3,2},{4,7},{5,4},{6,5},{7,6},{8,11},{9,8},{10,9... | collective-permute-start | bytes 12296 | tf_op jit(solution)/shard_map/ppermute | solution.py:259

commit v5 on v4

--- a/solution.py
+++ b/solution.py
@@ -19,7 +19,8 @@
 
 OWN, UP, DOWN, BELOW = range(4)
 BELOW_OWN, BELOW_UP, OWN_UP, OWN_UP_LATE, OWN_DOWN, UP_DOWN = range(6)
-TABLE = 8
+NEEDED = 6
+TABLE = 16
 LANES = 128
 TILE = 256
 CHUNKS = 4
@@ -48,14 +49,6 @@
     return [(b, a) for a, b in route]
 
 
-def unitize(values):
-    widened = values.astype(jnp.float32)
-    factor = lax.rsqrt(jnp.mean(widened * widened, axis=-1, keepdims=True) + epsilon) * (
-        1.0 / math.sqrt(values.shape[-1])
-    )
-    return (widened * factor).astype(jnp.bfloat16)
-
-
 def closeness_of(scores):
     return jax.nn.sigmoid(sharpness * (scores - threshold))
 
@@ -73,6 +66,17 @@
 
 def fold_sublanes(part, reduce):
     return reduce(part.reshape(part.shape[0] // 8, 8, part.shape[1]), axis=0)
+
+
+def normalise(raw_ref, out_ref):
+    rows, width = raw_ref.shape
+    step = rows // CHUNKS
+    for k in range(CHUNKS):
+        span = slice(k * step, (k + 1) * step)
+        widened = raw_ref[span, :].astype(jnp.float32)
+        mean = jnp.sum(fold_lanes(widened * widened, jnp.add), axis=1, keepdims=True) * (1.0 / width)
+        factor = lax.rsqrt(mean + epsilon) * (1.0 / math.sqrt(width))
+        out_ref[span, :] = (widened * factor).astype(jnp.bfloat16)
 
 
 def write_table(total, sizes_ref, place_ref, table_ref):
@@ -109,12 +113,16 @@
         OWN_DOWN: (cd == mine) & has_d & (x == RING - 1),
         UP_DOWN: (cu == cd) & has_d,
     }
+    flags[NEEDED + BELOW] = flags[BELOW_OWN] | below_up
+    flags[NEEDED + UP] = with_up | below_up | flags[UP_DOWN]
+    flags[NEEDED + DOWN] = flags[OWN_DOWN] | flags[UP_DOWN]
     for place, flag in flags.items():
         table_ref[place] = jnp.where(flag, jnp.int32(1), nought)
 
 
-def diag_kernel(total, sizes_ref, place_ref, x_ref, out_ref, table_ref):
+def diag_kernel(total, sizes_ref, place_ref, raw_ref, out_ref, table_ref, x_ref):
     rows = x_ref.shape[0]
+    normalise(raw_ref, x_ref)
     for c in range(rows // TILE):
         span = slice(c * TILE, (c + 1) * TILE)
         scores = score_block(x_ref[...], x_ref[span, :])
@@ -128,12 +136,14 @@
     write_table(total, sizes_ref, place_ref, table_ref)
 
 
-def pair_kernel(slots, given, pairs, table_ref, *refs):
+def pair_kernel(slots, given, pairs, arrived, table_ref, *refs):
     n = len(slots)
     held = dict(zip(given, refs))
     slab = dict(zip(slots, refs[len(given) :]))
     out = dict(zip(slots, refs[len(given) + n :]))
-    best, count = refs[len(given) + 2 * n :]
+    ready, best, count = refs[len(given) + 2 * n :]
+    raw, slab[arrived] = slab[arrived], ready
+    pl.when(table_ref[NEEDED + arrived] == 1)(functools.partial(normalise, raw, ready))
     at = {slot: k for k, slot in enumerate(slots)}
     rows = best.shape[2]
     best[...] = jnp.full(best.shape, floor_value, jnp.float32)
@@ -166,52 +176,27 @@
         out[slot][1:2, :] = near
 
 
-def normalise_kernel(x_ref, out_ref, raw, sems):
-    rows, width = raw.shape
-    step = rows // CHUNKS
-    spans = [slice(k * step, (k + 1) * step) for k in range(CHUNKS)]
-    copies = [pltpu.make_async_copy(x_ref.at[s, :], raw.at[s, :], sems.at[k]) for k, s in enumerate(spans)]
-    for copy in copies:
-        copy.start()
-    for copy, s in zip(copies, spans):
-        copy.wait()
-        widened = raw[s, :].astype(jnp.float32)
-        mean = jnp.sum(fold_lanes(widened * widened, jnp.add), axis=1, keepdims=True) * (1.0 / width)
-        factor = lax.rsqrt(mean + epsilon) * (1.0 / math.sqrt(width))
-        out_ref[s, :] = (widened * factor).astype(jnp.bfloat16)
-
-
 VMEM = pl.BlockSpec(memory_space=pltpu.VMEM)
 SMEM = pl.BlockSpec(memory_space=pltpu.SMEM)
 ANY = pl.BlockSpec(memory_space=pl.ANY)
 
 
-def pair_stats(table, stats, slabs, pairs):
+def pair_stats(table, stats, slabs, arrived, pairs):
     slots, given = list(slabs), list(stats)
     rows, width = slabs[OWN].shape
+    last = arrived == DOWN
+    ready = jax.ShapeDtypeStruct((rows, width), jnp.bfloat16)
+    kept = [pltpu.VMEM(ready.shape, ready.dtype)] if last else []
     outs = pl.pallas_call(
-        functools.partial(pair_kernel, slots, given, pairs),
+        functools.partial(pair_kernel, slots, given, pairs, arrived),
         in_specs=[SMEM] + [VMEM] * (len(given) + len(slots)),
-        out_specs=[VMEM] * len(slots),
-        out_shape=[jax.ShapeDtypeStruct((2, rows), jnp.float32)] * len(slots),
-        scratch_shapes=[pltpu.VMEM((len(slots), 8, rows), jnp.float32)] * 2,
+        out_specs=[VMEM] * (len(slots) + (not last)),
+        out_shape=[jax.ShapeDtypeStruct((2, rows), jnp.float32)] * len(slots) + ([] if last else [ready]),
+        scratch_shapes=kept + [pltpu.VMEM((len(slots), 8, rows), jnp.float32)] * 2,
         compiler_params=pltpu.CompilerParams(vmem_limit_bytes=20 * 1024 * 1024),
         cost_estimate=pl.CostEstimate(flops=2 * rows * rows * width, bytes_accessed=len(slots) * rows * width * 2, transcendentals=0),
     )(table, *[stats[s] for s in given], *[slabs[s] for s in slots])
-    return dict(zip(slots, outs))
-
-
-def normalised(embeddings):
-    rows, width = embeddings.shape
-    return pl.pallas_call(
-        normalise_kernel,
-        in_specs=[ANY],
-        out_specs=VMEM,
-        out_shape=jax.ShapeDtypeStruct((rows, width), jnp.bfloat16),
-        scratch_shapes=[pltpu.VMEM((rows, width), jnp.bfloat16), pltpu.SemaphoreType.DMA((CHUNKS,))],
-        compiler_params=pltpu.CompilerParams(vmem_limit_bytes=16 * 1024 * 1024),
-        cost_estimate=pl.CostEstimate(flops=4 * rows * width, bytes_accessed=2 * rows * width * 2, transcendentals=rows),
-    )(embeddings)
+    return dict(zip(slots, outs)), outs[-1]
 
 
 def diag_stats(total, cluster_sizes, place, own_slab):
@@ -219,10 +204,11 @@
     return pl.pallas_call(
         functools.partial(diag_kernel, total),
         in_specs=[SMEM, SMEM, VMEM],
-        out_specs=[VMEM, SMEM],
+        out_specs=[VMEM, SMEM, VMEM],
         out_shape=[
             jax.ShapeDtypeStruct((2, rows), jnp.float32),
             jax.ShapeDtypeStruct((TABLE,), jnp.int32),
+            jax.ShapeDtypeStruct((rows, width), jnp.bfloat16),
         ],
         compiler_params=pltpu.CompilerParams(vmem_limit_bytes=16 * 1024 * 1024),
         cost_estimate=pl.CostEstimate(flops=2 * rows * rows * width, bytes_accessed=rows * width * 2, transcendentals=0),
@@ -233,24 +219,25 @@
     below_route, up_route, down_route = routes(total)
 
     def body(embeddings, cluster_sizes):
-        normed = unitize(embeddings)
-        below = lax.ppermute(normed, AXES, below_route)
-        up = lax.ppermute(normed, AXES, up_route)
-        down = lax.ppermute(normed, AXES, down_route)
+        below = lax.ppermute(embeddings, AXES, below_route)
+        up = lax.ppermute(embeddings, AXES, up_route)
+        down = lax.ppermute(embeddings, AXES, down_route)
         p = lax.axis_index(AXES)
-        own, table = diag_stats(total, cluster_sizes, p[None].astype(jnp.int32), normed)
-        stats = pair_stats(table, {OWN: own}, {BELOW: below, OWN: normed}, [(BELOW_OWN, BELOW, OWN)])
-        stats = pair_stats(
+        own, table, normed = diag_stats(total, cluster_sizes, p[None].astype(jnp.int32), embeddings)
+        stats, below = pair_stats(table, {OWN: own}, {BELOW: below, OWN: normed}, BELOW, [(BELOW_OWN, BELOW, OWN)])
+        stats, up = pair_stats(
             table,
             stats,
             {BELOW: below, UP: up, OWN: normed},
+            UP,
             [(BELOW_UP, BELOW, UP), (OWN_UP, OWN, UP)],
         )
         for_below = stats.pop(BELOW)
-        stats = pair_stats(
+        stats, _ = pair_stats(
             table,
             stats,
             {DOWN: down, UP: up, OWN: normed},
+            DOWN,
             [(OWN_UP_LATE, OWN, UP), (OWN_DOWN, OWN, DOWN), (UP_DOWN, UP, DOWN)],
         )
         mine, for_up, for_down = stats[OWN], stats[UP], stats[DOWN]
@@ -259,10 +246,12 @@
         from_up = lax.ppermute(for_up, AXES, inverse(up_route))
         got_down = p >= 2
         got_below = p < total - RING
-        best = jnp.maximum(mine[0], from_up[0])
+        best, count = lax.optimization_barrier(
+            (jnp.maximum(mine[0], jnp.where(got_below, from_below[0], floor_value)), mine[1] + from_below[1])
+        )
+        best = jnp.maximum(best, from_up[0])
         best = jnp.maximum(best, jnp.where(got_down, from_down[0], floor_value))
-        best = jnp.maximum(best, jnp.where(got_below, from_below[0], floor_value))
-        return best, mine[1] + from_up[1] + from_down[1] + from_below[1]
+        return best, count + from_up[1] + from_down[1]
 
     return body
 

time: 57 us -> 54.9 us (0.963)
  waiting for transfers between devices: 13.4 us -> 10.8 us
  local copies, waits for them, and re-layouts: 0.01 us -> 1.9 us
  other arithmetic: 2.43 us -> 0.6 us
  starting transfers between devices: 33.3 us -> 34.1 us
    ppermute x3, waiting for transfers between devices: 12.2 us -> 10.1 us  [the longest x1 10.1 us: body(): below = lax.ppermute(embeddings, AXES, below_route)]
    unnamed x4, local copies, waits for them, and re-layouts: 0.01 us -> 1.9 us
    ppermute x1, starting transfers between devices: 5.15 us -> 6.81 us  [body(): from_up = lax.ppermute(for_up, AXES, inverse(up_route))]
    reduce_sum x1 -> x0, other arithmetic: 1.59 us -> none  [unitize(): jnp.mean(widened * widened, axis=-1, keepdims=True) + epsilon]
    ppermute x1, waiting for transfers between devices: 1.14 us -> 0.01 us  [body(): from_down = lax.ppermute(for_down, AXES, inverse(down_route))]
    ppermute x1, starting transfers between devices: 7.23 us -> 6.34 us  [body(): from_below = lax.ppermute(for_below, AXES, inverse(below_route))]
    ppermute x1, waiting for transfers between devices: 0.01 us -> 0.71 us  [body(): from_up = lax.ppermute(for_up, AXES, inverse(up_route))]
    pallas_call x3, Pallas kernels: 2.46 us -> 1.79 us  [pair_stats(): pl.pallas_call(functools.partial(pair_kernel, slots, given, pairs, arrive...]
where the time goes in v5:
time: 54.9 us; the launch traced here: 54.6 us
  starting transfers between devices  34.1 us (62%)
  waiting for transfers between devices  10.8 us (20%)
  Pallas kernels  6.43 us (12%)
  local copies, waits for them, and re-layouts  1.9 us (3%)
  between operations  0.76 us (1%)
  other arithmetic  0.6 us (1%)
    ppermute x1, starting transfers between devices, body(): down = lax.ppermute(embeddings, AXES, down_route)  11.5 us
    ppermute x1, waiting for transfers between devices, body(): below = lax.ppermute(embeddings, AXES, below_route)  10.1 us
    ppermute x1, starting transfers between devices, body(): from_up = lax.ppermute(for_up, AXES, inverse(up_route))  6.81 us
    ppermute x1, starting transfers between devices, body(): from_below = lax.ppermute(for_below, AXES, inverse(below_route))  6.34 us
    pallas_call x1, Pallas kernels, diag_stats(): pl.pallas_call(functools.partial(diag_kernel, total), in_specs=[SMEM, SME...  4.64 us
    ppermute x1, starting transfers between devices, body(): below = lax.ppermute(embeddings, AXES, below_route)  4.37 us
    ppermute x1, starting transfers between devices, body(): up = lax.ppermute(embeddings, AXES, up_route)  3.12 us
    ppermute x1, starting transfers between devices, body(): from_down = lax.ppermute(for_down, AXES, inverse(down_route))  1.92 us
  transfers between devices with their start and end apart: 6, of which 2 were waited for; matrix products, arithmetic and copies ran while one was open for 0% of the time, Pallas kernels for 12%

profile of v5, /device:TPU:1, one launch (start us, length us, event | category | flops | bytes accessed | tf_op | source)
XLA Modules:
  0.0 54.6 jit_solution(15502295216838048224)
XLA Ops:
  0.6 4.4 %collective-permute-start = (bf16[512,1024]{1,0:T(8,128)(2,1)}, bf16[512,1024]{1,0:T(8,128)(2,1)S(1)}, u32[]{:S(2)}, u32[]{:S(2)}) collective-permute-start(bf16[512,1024]{1,0:T(8,128)(2,1)} %raw_ref.1), channel_id=1, source_target_pairs={{0,4},{1,5},{2,6},{3,7},{4,8},{5,9},{6,10},{7,11},{8,12},{9,13},{1... | collective-permute-start | bytes 3145736 | tf_op jit(solution)/shard_map/ppermute | solution.py:222
  5.0 3.1 %collective-permute-start.1 = (bf16[512,1024]{1,0:T(8,128)(2,1)}, bf16[512,1024]{1,0:T(8,128)(2,1)S(1)}, u32[]{:S(2)}, u32[]{:S(2)}) collective-permute-start(bf16[512,1024]{1,0:T(8,128)(2,1)} %raw_ref.1), channel_id=1, source_target_pairs={{3,0},{0,1},{1,2},{2,3},{7,4},{4,5},{5,6},{6,7},{11,8},{8,9},{9,10... | collective-permute-start | bytes 3145736 | tf_op jit(solution)/shard_map/ppermute | solution.py:223
  8.1 11.5 %collective-permute-start.2 = (bf16[512,1024]{1,0:T(8,128)(2,1)}, bf16[512,1024]{1,0:T(8,128)(2,1)S(1)}, u32[]{:S(2)}, u32[]{:S(2)}) collective-permute-start(bf16[512,1024]{1,0:T(8,128)(2,1)} %raw_ref.1), channel_id=1, source_target_pairs={{5,0},{2,1},{3,2},{4,3},{9,4},{6,5},{7,6},{8,7},{13,8},{10,9},{11,... | collective-permute-start | bytes 3145736 | tf_op jit(solution)/shard_map/ppermute | solution.py:224
  19.7 0.0 copy-start.1
  19.7 0.7 %copy-done.1 = s32[170]{0:T(256)S(1)} copy-done((s32[170]{0:T(256)S(1)}, s32[170]{0:T(256)}, u32[]{:S(2)}) %copy-start.1) | copy-done | bytes 704
  20.4 0.0 copy-start
  20.4 1.2 %copy-done = bf16[512,1024]{1,0:T(8,128)(2,1)S(1)} copy-done((bf16[512,1024]{1,0:T(8,128)(2,1)S(1)}, bf16[512,1024]{1,0:T(8,128)(2,1)}, u32[]{:S(2)}) %copy-start) | copy-done | bytes 1048600
  21.6 4.6 %shard_map.41 = (f32[2,512]{1,0:T(2,128)S(1)}, s32[16]{0:T(128)S(1)}, bf16[512,1024]{1,0:T(8,128)(2,1)S(1)}) custom-call(s32[170]{0:T(256)S(1)} %copy-done.1, s32[1]{0:T(128)} %bitcast.place_ref, bf16[512,1024]{1,0:T(8,128)(2,1)S(1)} %copy-done), custom_call_target="tpu_custom_call" | custom-call | flops 536870912 | bytes 1048576 | tf_op jit(solution)/shard_map/pallas_call | solution.py:204
  26.2 10.1 %collective-permute-done.refs_1_ = bf16[512,1024]{1,0:T(8,128)(2,1)S(1)} collective-permute-done((bf16[512,1024]{1,0:T(8,128)(2,1)}, bf16[512,1024]{1,0:T(8,128)(2,1)S(1)}, u32[]{:S(2)}, u32[]{:S(2)}) %collective-permute-start) | collective-permute-done | bytes 1048608 | tf_op jit(solution)/shard_map/ppermute | solution.py:222
  36.3 0.6 %shard_map.42 = (f32[2,512]{1,0:T(2,128)S(1)}, f32[2,512]{1,0:T(2,128)S(1)}, bf16[512,1024]{1,0:T(8,128)(2,1)S(1)}) custom-call(s32[16]{0:T(128)S(1)} %get-tuple-element.17.table_ref, f32[2,512]{1,0:T(2,128)S(1)} %get-tuple-element.18.refs_0_, bf16[512,1024]{1,0:T(8,128)(2,1)S(1)} %collective-permute-done.refs_1_, ...), custom_call_target="tpu_custom_call" | custom-call | flops 536870912 | bytes 2097152 | tf_op jit(solution)/shard_map/pallas_call | solution.py:190
  36.9 0.0 collective-permute-done.1.refs_3_
  36.9 0.6 %shard_map.43 = (f32[2,512]{1,0:T(2,128)S(1)}, f32[2,512]{1,0:T(2,128)S(1)}, f32[2,512]{1,0:T(2,128)S(1)}, bf16[512,1024]{1,0:T(8,128)(2,1)S(1)}) custom-call(s32[16]{0:T(128)S(1)} %get-tuple-element.17.table_ref, f32[2,512]{1,0:T(2,128)S(1)} %get-tuple-element.20.refs_0_, f32[2,512]{1,0:T(2,128)S(1)} %get-tuple-element.21.refs_1_, ...), custom_call_target="tpu_custom_call" | custom-call | flops 536870912 | bytes 3145728 | tf_op jit(solution)/shard_map/pallas_call | solution.py:190
  37.5 6.3 %collective-permute-start.3 = (f32[2,512]{1,0:T(2,128)S(1)}, f32[2,512]{1,0:T(2,128)S(1)}, u32[]{:S(2)}, u32[]{:S(2)}) collective-permute-start(f32[2,512]{1,0:T(2,128)S(1)} %get-tuple-element.27), channel_id=1, source_target_pairs={{4,0},{5,1},{6,2},{7,3},{8,4},{9,5},{10,6},{11,7},{12,8},{13,9},{1... | collective-permute-start | bytes 12296 | tf_op jit(solution)/shard_map/ppermute | solution.py:244
  43.9 0.0 collective-permute-done.2.refs_2_
  43.9 0.6 %shard_map.44 = (f32[2,512]{1,0:T(2,128)S(1)}, f32[2,512]{1,0:T(2,128)S(1)}, f32[2,512]{1,0:T(2,128)S(1)}) custom-call(s32[16]{0:T(128)S(1)} %get-tuple-element.17.table_ref, f32[2,512]{1,0:T(2,128)S(1)} %get-tuple-element.23.refs_0_, f32[2,512]{1,0:T(2,128)S(1)} %get-tuple-element.24.refs_1_, bf16[512,1024]{1,0:T(8,128)(2,1)S(1)} %collective-permute-done.2.refs_2_, ...), custom_call_target="tpu_custom_call" | custom-call | flops 536870912 | bytes 3145728 | tf_op jit(solution)/shard_map/pallas_call | solution.py:190
  44.5 1.9 %collective-permute-start.5 = (f32[2,512]{1,0:T(2,128)S(1)}, f32[2,512]{1,0:T(2,128)S(1)}, u32[]{:S(2)}, u32[]{:S(2)}) collective-permute-start(f32[2,512]{1,0:T(2,128)S(1)} %get-tuple-element.30), channel_id=1, source_target_pairs={{0,5},{1,2},{2,3},{3,4},{4,9},{5,6},{6,7},{7,8},{8,13},{9,10},{10,... | collective-permute-start | bytes 12296 | tf_op jit(solution)/shard_map/ppermute | solution.py:245
  46.4 6.8 %collective-permute-start.4 = (f32[2,512]{1,0:T(2,128)S(1)}, f32[2,512]{1,0:T(2,128)S(1)}, u32[]{:S(2)}, u32[]{:S(2)}) collective-permute-start(f32[2,512]{1,0:T(2,128)S(1)} %get-tuple-element.29), channel_id=1, source_target_pairs={{0,3},{1,0},{2,1},{3,2},{4,7},{5,4},{6,5},{7,6},{8,11},{9,8},{10,9... | collective-permute-start | bytes 12296 | tf_op jit(solution)/shard_map/ppermute | solution.py:246
  53.3 0.0 collective-permute-done.3
  53.3 0.7 %collective-permute-done.4 = f32[2,512]{1,0:T(2,128)S(1)} collective-permute-done((f32[2,512]{1,0:T(2,128)S(1)}, f32[2,512]{1,0:T(2,128)S(1)}, u32[]{:S(2)}, u32[]{:S(2)}) %collective-permute-start.4) | collective-permute-done | bytes 4128 | tf_op jit(solution)/shard_map/ppermute | solution.py:246
  54.0 0.0 collective-permute-done.5
  54.0 0.6 %add_add_fusion = (f32[512]{0:T(512)}, f32[512]{0:T(512)}) fusion(f32[512]{0:T(512)S(1)} %bitcast.9, f32[512]{0:T(512)S(1)} %bitcast.7, f32[512]{0:T(512)S(1)} %bitcast.11, f32[512]{0:T(512)S(1)} %bitcast.10, f32[512]{0:T(512)S(1)} %bitcast.8, f32[512]{0:T(512)S(1)} %bitcast.12), kind=kLoop, calls=%fused_computation.4 | loop fusion | flops 2048 | bytes 16384 | tf_op jit(solution)/shard_map/add | solution.py:254
  (3 shorter events, 0.0 us)
Async XLA Ops:
  0.6 35.7 %collective-permute-start = (bf16[512,1024]{1,0:T(8,128)(2,1)}, bf16[512,1024]{1,0:T(8,128)(2,1)S(1)}, u32[]{:S(2)}, u32[]{:S(2)}) collective-permute-start(bf16[512,1024]{1,0:T(8,128)(2,1)} %raw_ref.1), channel_id=1, source_target_pairs={{0,4},{1,5},{2,6},{3,7},{4,8},{5,9},{6,10},{7,11},{8,12},{9,13},{1... | collective-permute-start | bytes 3145736 | tf_op jit(solution)/shard_map/ppermute | solution.py:222
  5.0 31.9 %collective-permute-start.1 = (bf16[512,1024]{1,0:T(8,128)(2,1)}, bf16[512,1024]{1,0:T(8,128)(2,1)S(1)}, u32[]{:S(2)}, u32[]{:S(2)}) collective-permute-start(bf16[512,1024]{1,0:T(8,128)(2,1)} %raw_ref.1), channel_id=1, source_target_pairs={{3,0},{0,1},{1,2},{2,3},{7,4},{4,5},{5,6},{6,7},{11,8},{8,9},{9,10... | collective-permute-start | bytes 3145736 | tf_op jit(solution)/shard_map/ppermute | solution.py:223
  8.1 35.8 %collective-permute-start.2 = (bf16[512,1024]{1,0:T(8,128)(2,1)}, bf16[512,1024]{1,0:T(8,128)(2,1)S(1)}, u32[]{:S(2)}, u32[]{:S(2)}) collective-permute-start(bf16[512,1024]{1,0:T(8,128)(2,1)} %raw_ref.1), channel_id=1, source_target_pairs={{5,0},{2,1},{3,2},{4,3},{9,4},{6,5},{7,6},{8,7},{13,8},{10,9},{11,... | collective-permute-start | bytes 3145736 | tf_op jit(solution)/shard_map/ppermute | solution.py:224
  19.7 0.7 %copy-start.1 = (s32[170]{0:T(256)S(1)}, s32[170]{0:T(256)}, u32[]{:S(2)}) copy-start(s32[170]{0:T(256)} %sizes_ref.1) | copy-start | bytes 2044
  20.4 1.2 %copy-start = (bf16[512,1024]{1,0:T(8,128)(2,1)S(1)}, bf16[512,1024]{1,0:T(8,128)(2,1)}, u32[]{:S(2)}) copy-start(bf16[512,1024]{1,0:T(8,128)(2,1)} %raw_ref.1) | copy-start | bytes 3145732
  37.5 15.7 %collective-permute-start.3 = (f32[2,512]{1,0:T(2,128)S(1)}, f32[2,512]{1,0:T(2,128)S(1)}, u32[]{:S(2)}, u32[]{:S(2)}) collective-permute-start(f32[2,512]{1,0:T(2,128)S(1)} %get-tuple-element.27), channel_id=1, source_target_pairs={{4,0},{5,1},{6,2},{7,3},{8,4},{9,5},{10,6},{11,7},{12,8},{13,9},{1... | collective-permute-start | bytes 12296 | tf_op jit(solution)/shard_map/ppermute | solution.py:244
  44.5 9.5 %collective-permute-start.5 = (f32[2,512]{1,0:T(2,128)S(1)}, f32[2,512]{1,0:T(2,128)S(1)}, u32[]{:S(2)}, u32[]{:S(2)}) collective-permute-start(f32[2,512]{1,0:T(2,128)S(1)} %get-tuple-element.30), channel_id=1, source_target_pairs={{0,5},{1,2},{2,3},{3,4},{4,9},{5,6},{6,7},{7,8},{8,13},{9,10},{10,... | collective-permute-start | bytes 12296 | tf_op jit(solution)/shard_map/ppermute | solution.py:245
  46.4 7.6 %collective-permute-start.4 = (f32[2,512]{1,0:T(2,128)S(1)}, f32[2,512]{1,0:T(2,128)S(1)}, u32[]{:S(2)}, u32[]{:S(2)}) collective-permute-start(f32[2,512]{1,0:T(2,128)S(1)} %get-tuple-element.29), channel_id=1, source_target_pairs={{0,3},{1,0},{2,1},{3,2},{4,7},{5,4},{6,5},{7,6},{8,11},{9,8},{10,9... | collective-permute-start | bytes 12296 | tf_op jit(solution)/shard_map/ppermute | solution.py:246

commit v6 on v5

--- a/solution.py
+++ b/solution.py
@@ -18,12 +18,11 @@
 floor_value = -2.0
 
 OWN, UP, DOWN, BELOW = range(4)
-BELOW_OWN, BELOW_UP, OWN_UP, OWN_UP_LATE, OWN_DOWN, UP_DOWN = range(6)
-NEEDED = 6
-TABLE = 16
+BELOW_OWN, BELOW_ONLY, BELOW_UP, OWN_UP, UP_ONLY, OWN_UP_LATE, OWN_DOWN, UP_DOWN, BOTH_DOWN = range(9)
+MASK = (8, 128)
 LANES = 128
 TILE = 256
-CHUNKS = 4
+CHUNK = 128
 
 
 def upper_source(p):
@@ -68,18 +67,17 @@
     return reduce(part.reshape(part.shape[0] // 8, 8, part.shape[1]), axis=0)
 
 
-def normalise(raw_ref, out_ref):
-    rows, width = raw_ref.shape
-    step = rows // CHUNKS
-    for k in range(CHUNKS):
-        span = slice(k * step, (k + 1) * step)
+def normalise(raw_ref, out_ref, start, stop):
+    width = raw_ref.shape[1]
+    for k in range(start, stop, CHUNK):
+        span = slice(k, k + CHUNK)
         widened = raw_ref[span, :].astype(jnp.float32)
         mean = jnp.sum(fold_lanes(widened * widened, jnp.add), axis=1, keepdims=True) * (1.0 / width)
         factor = lax.rsqrt(mean + epsilon) * (1.0 / math.sqrt(width))
         out_ref[span, :] = (widened * factor).astype(jnp.bfloat16)
 
 
-def write_table(total, sizes_ref, place_ref, table_ref):
+def write_mask(total, sizes_ref, place_ref, mask_ref):
     p = place_ref[0]
     x = lax.rem(p, RING)
     qu = jnp.where(x == 0, p + RING - 1, p - 1)
@@ -105,24 +103,29 @@
     has_z = qz >= 0
     with_up = cu == mine
     below_up = (cz == cu) & has_z & (x > 0)
+    below_own = (cz == mine) & has_z
+    own_down = (cd == mine) & has_d & (x == RING - 1)
+    up_down = (cu == cd) & has_d
     flags = {
-        BELOW_OWN: (cz == mine) & has_z,
+        BELOW_OWN: below_own,
+        BELOW_ONLY: below_up & ~below_own,
         BELOW_UP: below_up,
         OWN_UP: with_up & ~below_up,
+        UP_ONLY: up_down & ~with_up & ~below_up,
         OWN_UP_LATE: with_up & below_up,
-        OWN_DOWN: (cd == mine) & has_d & (x == RING - 1),
-        UP_DOWN: (cu == cd) & has_d,
+        OWN_DOWN: own_down & ~up_down,
+        UP_DOWN: up_down & ~own_down,
+        BOTH_DOWN: own_down & up_down,
     }
-    flags[NEEDED + BELOW] = flags[BELOW_OWN] | below_up
-    flags[NEEDED + UP] = with_up | below_up | flags[UP_DOWN]
-    flags[NEEDED + DOWN] = flags[OWN_DOWN] | flags[UP_DOWN]
+    bits = nought
     for place, flag in flags.items():
-        table_ref[place] = jnp.where(flag, jnp.int32(1), nought)
-
-
-def diag_kernel(total, sizes_ref, place_ref, raw_ref, out_ref, table_ref, x_ref):
+        bits = bits + jnp.where(flag, jnp.int32(1 << place), nought)
+    mask_ref[...] = jnp.full(MASK, bits.astype(jnp.float32), jnp.float32)
+
+
+def diag_kernel(total, sizes_ref, place_ref, raw_ref, out_ref, mask_ref, x_ref):
     rows = x_ref.shape[0]
-    normalise(raw_ref, x_ref)
+    normalise(raw_ref, x_ref, 0, rows)
     for c in range(rows // TILE):
         span = slice(c * TILE, (c + 1) * TILE)
         scores = score_block(x_ref[...], x_ref[span, :])
@@ -133,38 +136,42 @@
         high = jnp.where(self_pair, floor_value, scores)
         out_ref[0:1, span] = jnp.max(high, axis=0, keepdims=True)
         out_ref[1:2, span] = jnp.sum(near, axis=0, keepdims=True)
-    write_table(total, sizes_ref, place_ref, table_ref)
-
-
-def pair_kernel(slots, given, pairs, arrived, table_ref, *refs):
+    write_mask(total, sizes_ref, place_ref, mask_ref)
+
+
+def pair_kernel(slots, given, cases, arrived, mask_ref, *refs):
     n = len(slots)
     held = dict(zip(given, refs))
     slab = dict(zip(slots, refs[len(given) :]))
     out = dict(zip(slots, refs[len(given) + n :]))
     ready, best, count = refs[len(given) + 2 * n :]
     raw, slab[arrived] = slab[arrived], ready
-    pl.when(table_ref[NEEDED + arrived] == 1)(functools.partial(normalise, raw, ready))
     at = {slot: k for k, slot in enumerate(slots)}
     rows = best.shape[2]
     best[...] = jnp.full(best.shape, floor_value, jnp.float32)
     count[...] = jnp.zeros(count.shape, jnp.float32)
 
-    def score_pair(i, j):
-        high_rows = near_rows = None
-        for c in range(rows // TILE):
-            span = slice(c * TILE, (c + 1) * TILE)
-            scores = score_block(slab[i][...], slab[j][span, :])
-            near = closeness_of(scores)
-            best[at[j], :, span] = jnp.maximum(best[at[j], :, span], fold_sublanes(scores, jnp.max))
-            count[at[j], :, span] = count[at[j], :, span] + fold_sublanes(near, jnp.sum)
-            high_part, near_part = fold_lanes(scores, jnp.maximum), fold_lanes(near, jnp.add)
-            high_rows = high_part if high_rows is None else jnp.maximum(high_rows, high_part)
-            near_rows = near_part if near_rows is None else near_rows + near_part
-        best[at[i]] = jnp.maximum(best[at[i]], fold_sublanes(high_rows.T, jnp.max))
-        count[at[i]] = count[at[i]] + fold_sublanes(near_rows.T, jnp.sum)
-
-    for flag, i, j in pairs:
-        pl.when(table_ref[flag] == 1)(functools.partial(score_pair, i, j))
+    def run(lefts, j):
+        high_rows, near_rows = {}, {}
+        for start in range(0, rows, TILE):
+            span = slice(start, start + TILE)
+            if j == arrived:
+                normalise(raw, ready, start, start + TILE)
+            for i in lefts:
+                scores = score_block(slab[i][...], slab[j][span, :])
+                near = closeness_of(scores)
+                best[at[j], :, span] = jnp.maximum(best[at[j], :, span], fold_sublanes(scores, jnp.max))
+                count[at[j], :, span] = count[at[j], :, span] + fold_sublanes(near, jnp.sum)
+                high_part, near_part = fold_lanes(scores, jnp.maximum), fold_lanes(near, jnp.add)
+                high_rows[i] = high_part if start == 0 else jnp.maximum(high_rows[i], high_part)
+                near_rows[i] = near_part if start == 0 else near_rows[i] + near_part
+        for i in lefts:
+            best[at[i]] = jnp.maximum(best[at[i]], fold_sublanes(high_rows[i].T, jnp.max))
+            count[at[i]] = count[at[i]] + fold_sublanes(near_rows[i].T, jnp.sum)
+
+    bits = jnp.max(mask_ref[...]).astype(jnp.int32)
+    for flag, lefts, j in cases:
+        pl.when((bits & (1 << flag)) != 0)(functools.partial(run, lefts, j))
 
     for slot in slots:
         high = jnp.max(best[at[slot]], axis=0, keepdims=True)
@@ -181,21 +188,21 @@
 ANY = pl.BlockSpec(memory_space=pl.ANY)
 
 
-def pair_stats(table, stats, slabs, arrived, pairs):
+def pair_stats(mask, stats, slabs, arrived, cases):
     slots, given = list(slabs), list(stats)
     rows, width = slabs[OWN].shape
     last = arrived == DOWN
     ready = jax.ShapeDtypeStruct((rows, width), jnp.bfloat16)
     kept = [pltpu.VMEM(ready.shape, ready.dtype)] if last else []
     outs = pl.pallas_call(
-        functools.partial(pair_kernel, slots, given, pairs, arrived),
-        in_specs=[SMEM] + [VMEM] * (len(given) + len(slots)),
+        functools.partial(pair_kernel, slots, given, cases, arrived),
+        in_specs=[VMEM] * (1 + len(given) + len(slots)),
         out_specs=[VMEM] * (len(slots) + (not last)),
         out_shape=[jax.ShapeDtypeStruct((2, rows), jnp.float32)] * len(slots) + ([] if last else [ready]),
         scratch_shapes=kept + [pltpu.VMEM((len(slots), 8, rows), jnp.float32)] * 2,
         compiler_params=pltpu.CompilerParams(vmem_limit_bytes=20 * 1024 * 1024),
         cost_estimate=pl.CostEstimate(flops=2 * rows * rows * width, bytes_accessed=len(slots) * rows * width * 2, transcendentals=0),
-    )(table, *[stats[s] for s in given], *[slabs[s] for s in slots])
+    )(mask, *[stats[s] for s in given], *[slabs[s] for s in slots])
     return dict(zip(slots, outs)), outs[-1]
 
 
@@ -204,10 +211,10 @@
     return pl.pallas_call(
         functools.partial(diag_kernel, total),
         in_specs=[SMEM, SMEM, VMEM],
-        out_specs=[VMEM, SMEM, VMEM],
+        out_specs=[VMEM, VMEM, VMEM],
         out_shape=[
             jax.ShapeDtypeStruct((2, rows), jnp.float32),
-            jax.ShapeDtypeStruct((TABLE,), jnp.int32),
+            jax.ShapeDtypeStruct(MASK, jnp.float32),
             jax.ShapeDtypeStruct((rows, width), jnp.bfloat16),
         ],
         compiler_params=pltpu.CompilerParams(vmem_limit_bytes=16 * 1024 * 1024),
@@ -223,22 +230,33 @@
         up = lax.ppermute(embeddings, AXES, up_route)
         down = lax.ppermute(embeddings, AXES, down_route)
         p = lax.axis_index(AXES)
-        own, table, normed = diag_stats(total, cluster_sizes, p[None].astype(jnp.int32), embeddings)
-        stats, below = pair_stats(table, {OWN: own}, {BELOW: below, OWN: normed}, BELOW, [(BELOW_OWN, BELOW, OWN)])
+        own, mask, normed = diag_stats(total, cluster_sizes, p[None].astype(jnp.int32), embeddings)
+        stats, below = pair_stats(
+            mask,
+            {OWN: own},
+            {BELOW: below, OWN: normed},
+            BELOW,
+            [(BELOW_OWN, (OWN,), BELOW), (BELOW_ONLY, (), BELOW)],
+        )
         stats, up = pair_stats(
-            table,
+            mask,
             stats,
             {BELOW: below, UP: up, OWN: normed},
             UP,
-            [(BELOW_UP, BELOW, UP), (OWN_UP, OWN, UP)],
+            [(BELOW_UP, (BELOW,), UP), (OWN_UP, (OWN,), UP), (UP_ONLY, (), UP)],
         )
         for_below = stats.pop(BELOW)
         stats, _ = pair_stats(
-            table,
+            mask,
             stats,
             {DOWN: down, UP: up, OWN: normed},
             DOWN,
-            [(OWN_UP_LATE, OWN, UP), (OWN_DOWN, OWN, DOWN), (UP_DOWN, UP, DOWN)],
+            [
+                (OWN_UP_LATE, (OWN,), UP),
+                (OWN_DOWN, (OWN,), DOWN),
+                (UP_DOWN, (UP,), DOWN),
+                (BOTH_DOWN, (OWN, UP), DOWN),
+            ],
         )
         mine, for_up, for_down = stats[OWN], stats[UP], stats[DOWN]
         from_below = lax.ppermute(for_below, AXES, inverse(below_route))

time: 54.9 us -> 54.4 us (level)
  starting transfers between devices: 34.1 us -> 31.9 us
  waiting for transfers between devices: 10.8 us -> 12.8 us
    ppermute x1, starting transfers between devices: 6.81 us -> 4.16 us  [body(): from_up = lax.ppermute(for_up, AXES, inverse(up_route))]
    ppermute x1, waiting for transfers between devices: 0.01 us -> 1.41 us  [body(): from_down = lax.ppermute(for_down, AXES, inverse(down_route))]
    pallas_call x1, Pallas kernels: 4.64 us -> 4.05 us  [diag_stats(): pl.pallas_call(functools.partial(diag_kernel, total), in_specs=[SMEM, SME...]
    ppermute x1, waiting for transfers between devices: 10.1 us -> 10.7 us  [body(): below = lax.ppermute(embeddings, AXES, below_route)]
  transfers between devices with their start and end apart: 6 -> 6, of which waited for: 2 -> 3; matrix products, arithmetic and copies ran while one was open for 0% -> 0% of each run, Pallas kernels for 12% -> 11%
where the time goes in v6:
time: 54.4 us; the launch traced here: 54.1 us
  starting transfers between devices  31.9 us (59%)
  waiting for transfers between devices  12.8 us (24%)
  Pallas kernels  6.13 us (11%)
  local copies, waits for them, and re-layouts  1.9 us (3%)
  between operations  0.76 us (1%)
  other arithmetic  0.6 us (1%)
    ppermute x1, starting transfers between devices, body(): down = lax.ppermute(embeddings, AXES, down_route)  11.5 us
    ppermute x1, waiting for transfers between devices, body(): below = lax.ppermute(embeddings, AXES, below_route)  10.7 us
    ppermute x1, starting transfers between devices, body(): from_below = lax.ppermute(for_below, AXES, inverse(below_route))  6.76 us
    ppermute x1, starting transfers between devices, body(): below = lax.ppermute(embeddings, AXES, below_route)  4.37 us
    ppermute x1, starting transfers between devices, body(): from_up = lax.ppermute(for_up, AXES, inverse(up_route))  4.16 us
    pallas_call x1, Pallas kernels, diag_stats(): pl.pallas_call(functools.partial(diag_kernel, total), in_specs=[SMEM, SME...  4.05 us
    ppermute x1, starting transfers between devices, body(): up = lax.ppermute(embeddings, AXES, up_route)  3.12 us
    pallas_call x3, Pallas kernels, pair_stats(): pl.pallas_call(functools.partial(pair_kernel, slots, given, cases, arrive...  2.08 us
  transfers between devices with their start and end apart: 6, of which 3 were waited for; matrix products, arithmetic and copies ran while one was open for 0% of the time, Pallas kernels for 11%

profile of v6, /device:TPU:1, one launch (start us, length us, event | category | flops | bytes accessed | tf_op | source)
XLA Modules:
  0.0 54.1 jit_solution(17704692116832029622)
XLA Ops:
  0.6 4.4 %collective-permute-start = (bf16[512,1024]{1,0:T(8,128)(2,1)}, bf16[512,1024]{1,0:T(8,128)(2,1)S(1)}, u32[]{:S(2)}, u32[]{:S(2)}) collective-permute-start(bf16[512,1024]{1,0:T(8,128)(2,1)} %raw_ref.1), channel_id=1, source_target_pairs={{0,4},{1,5},{2,6},{3,7},{4,8},{5,9},{6,10},{7,11},{8,12},{9,13},{1... | collective-permute-start | bytes 3145736 | tf_op jit(solution)/shard_map/ppermute | solution.py:229
  5.0 3.1 %collective-permute-start.1 = (bf16[512,1024]{1,0:T(8,128)(2,1)}, bf16[512,1024]{1,0:T(8,128)(2,1)S(1)}, u32[]{:S(2)}, u32[]{:S(2)}) collective-permute-start(bf16[512,1024]{1,0:T(8,128)(2,1)} %raw_ref.1), channel_id=1, source_target_pairs={{3,0},{0,1},{1,2},{2,3},{7,4},{4,5},{5,6},{6,7},{11,8},{8,9},{9,10... | collective-permute-start | bytes 3145736 | tf_op jit(solution)/shard_map/ppermute | solution.py:230
  8.1 11.5 %collective-permute-start.2 = (bf16[512,1024]{1,0:T(8,128)(2,1)}, bf16[512,1024]{1,0:T(8,128)(2,1)S(1)}, u32[]{:S(2)}, u32[]{:S(2)}) collective-permute-start(bf16[512,1024]{1,0:T(8,128)(2,1)} %raw_ref.1), channel_id=1, source_target_pairs={{5,0},{2,1},{3,2},{4,3},{9,4},{6,5},{7,6},{8,7},{13,8},{10,9},{11,... | collective-permute-start | bytes 3145736 | tf_op jit(solution)/shard_map/ppermute | solution.py:231
  19.7 0.0 copy-start.1
  19.7 0.7 %copy-done.1 = s32[170]{0:T(256)S(1)} copy-done((s32[170]{0:T(256)S(1)}, s32[170]{0:T(256)}, u32[]{:S(2)}) %copy-start.1) | copy-done | bytes 704
  20.4 0.0 copy-start
  20.4 1.2 %copy-done = bf16[512,1024]{1,0:T(8,128)(2,1)S(1)} copy-done((bf16[512,1024]{1,0:T(8,128)(2,1)S(1)}, bf16[512,1024]{1,0:T(8,128)(2,1)}, u32[]{:S(2)}) %copy-start) | copy-done | bytes 1048600
  21.6 4.1 %shard_map.41 = (f32[2,512]{1,0:T(2,128)S(1)}, f32[8,128]{1,0:T(8,128)S(1)}, bf16[512,1024]{1,0:T(8,128)(2,1)S(1)}) custom-call(s32[170]{0:T(256)S(1)} %copy-done.1, s32[1]{0:T(128)} %bitcast.place_ref, bf16[512,1024]{1,0:T(8,128)(2,1)S(1)} %copy-done), custom_call_target="tpu_custom_call" | custom-call | flops 536870912 | bytes 1048576 | tf_op jit(solution)/shard_map/pallas_call | solution.py:211
  25.6 10.7 %collective-permute-done.refs_1_ = bf16[512,1024]{1,0:T(8,128)(2,1)S(1)} collective-permute-done((bf16[512,1024]{1,0:T(8,128)(2,1)}, bf16[512,1024]{1,0:T(8,128)(2,1)S(1)}, u32[]{:S(2)}, u32[]{:S(2)}) %collective-permute-start) | collective-permute-done | bytes 1048608 | tf_op jit(solution)/shard_map/ppermute | solution.py:229
  36.3 0.2 shard_map.42
  36.5 0.0 collective-permute-done.1.refs_3_
  36.5 0.5 shard_map.43
  37.0 6.8 %collective-permute-start.3 = (f32[2,512]{1,0:T(2,128)S(1)}, f32[2,512]{1,0:T(2,128)S(1)}, u32[]{:S(2)}, u32[]{:S(2)}) collective-permute-start(f32[2,512]{1,0:T(2,128)S(1)} %get-tuple-element.27), channel_id=1, source_target_pairs={{4,0},{5,1},{6,2},{7,3},{8,4},{9,5},{10,6},{11,7},{12,8},{13,9},{1... | collective-permute-start | bytes 12296 | tf_op jit(solution)/shard_map/ppermute | solution.py:262
  43.8 0.0 collective-permute-done.2.refs_2_
  43.8 1.4 %shard_map.44 = (f32[2,512]{1,0:T(2,128)S(1)}, f32[2,512]{1,0:T(2,128)S(1)}, f32[2,512]{1,0:T(2,128)S(1)}) custom-call(f32[8,128]{1,0:T(8,128)S(1)} %get-tuple-element.17.mask_ref, f32[2,512]{1,0:T(2,128)S(1)} %get-tuple-element.23.refs_0_, f32[2,512]{1,0:T(2,128)S(1)} %get-tuple-element.24.refs_1_, bf16[512,1024]{1,0:T(8,128)(2,1)S(1)} %collective-permute-done.2.refs_2_, ...), custom_call_target="tpu_custom_call" | custom-call | flops 536870912 | bytes 3145728 | tf_op jit(solution)/shard_map/pallas_call | solution.py:197
  45.2 1.9 %collective-permute-start.5 = (f32[2,512]{1,0:T(2,128)S(1)}, f32[2,512]{1,0:T(2,128)S(1)}, u32[]{:S(2)}, u32[]{:S(2)}) collective-permute-start(f32[2,512]{1,0:T(2,128)S(1)} %get-tuple-element.30), channel_id=1, source_target_pairs={{0,5},{1,2},{2,3},{3,4},{4,9},{5,6},{6,7},{7,8},{8,13},{9,10},{10,... | collective-permute-start | bytes 12296 | tf_op jit(solution)/shard_map/ppermute | solution.py:263
  47.2 4.2 %collective-permute-start.4 = (f32[2,512]{1,0:T(2,128)S(1)}, f32[2,512]{1,0:T(2,128)S(1)}, u32[]{:S(2)}, u32[]{:S(2)}) collective-permute-start(f32[2,512]{1,0:T(2,128)S(1)} %get-tuple-element.29), channel_id=1, source_target_pairs={{0,3},{1,0},{2,1},{3,2},{4,7},{5,4},{6,5},{7,6},{8,11},{9,8},{10,9... | collective-permute-start | bytes 12296 | tf_op jit(solution)/shard_map/ppermute | solution.py:264
  51.3 0.0 collective-permute-done.3
  51.4 0.7 %collective-permute-done.4 = f32[2,512]{1,0:T(2,128)S(1)} collective-permute-done((f32[2,512]{1,0:T(2,128)S(1)}, f32[2,512]{1,0:T(2,128)S(1)}, u32[]{:S(2)}, u32[]{:S(2)}) %collective-permute-start.4) | collective-permute-done | bytes 4128 | tf_op jit(solution)/shard_map/ppermute | solution.py:264
  52.1 1.4 %collective-permute-done.5 = f32[2,512]{1,0:T(2,128)S(1)} collective-permute-done((f32[2,512]{1,0:T(2,128)S(1)}, f32[2,512]{1,0:T(2,128)S(1)}, u32[]{:S(2)}, u32[]{:S(2)}) %collective-permute-start.5) | collective-permute-done | bytes 4128 | tf_op jit(solution)/shard_map/ppermute | solution.py:263
  53.5 0.6 %add_add_fusion = (f32[512]{0:T(512)}, f32[512]{0:T(512)}) fusion(f32[512]{0:T(512)S(1)} %bitcast.9, f32[512]{0:T(512)S(1)} %bitcast.7, f32[512]{0:T(512)S(1)} %bitcast.11, f32[512]{0:T(512)S(1)} %bitcast.10, f32[512]{0:T(512)S(1)} %bitcast.8, f32[512]{0:T(512)S(1)} %bitcast.12), kind=kLoop, calls=%fused_computation.4 | loop fusion | flops 2048 | bytes 16384 | tf_op jit(solution)/shard_map/add | solution.py:272
  (3 shorter events, 0.0 us)
Async XLA Ops:
  0.6 35.7 %collective-permute-start = (bf16[512,1024]{1,0:T(8,128)(2,1)}, bf16[512,1024]{1,0:T(8,128)(2,1)S(1)}, u32[]{:S(2)}, u32[]{:S(2)}) collective-permute-start(bf16[512,1024]{1,0:T(8,128)(2,1)} %raw_ref.1), channel_id=1, source_target_pairs={{0,4},{1,5},{2,6},{3,7},{4,8},{5,9},{6,10},{7,11},{8,12},{9,13},{1... | collective-permute-start | bytes 3145736 | tf_op jit(solution)/shard_map/ppermute | solution.py:229
  5.0 31.5 %collective-permute-start.1 = (bf16[512,1024]{1,0:T(8,128)(2,1)}, bf16[512,1024]{1,0:T(8,128)(2,1)S(1)}, u32[]{:S(2)}, u32[]{:S(2)}) collective-permute-start(bf16[512,1024]{1,0:T(8,128)(2,1)} %raw_ref.1), channel_id=1, source_target_pairs={{3,0},{0,1},{1,2},{2,3},{7,4},{4,5},{5,6},{6,7},{11,8},{8,9},{9,10... | collective-permute-start | bytes 3145736 | tf_op jit(solution)/shard_map/ppermute | solution.py:230
  8.1 35.7 %collective-permute-start.2 = (bf16[512,1024]{1,0:T(8,128)(2,1)}, bf16[512,1024]{1,0:T(8,128)(2,1)S(1)}, u32[]{:S(2)}, u32[]{:S(2)}) collective-permute-start(bf16[512,1024]{1,0:T(8,128)(2,1)} %raw_ref.1), channel_id=1, source_target_pairs={{5,0},{2,1},{3,2},{4,3},{9,4},{6,5},{7,6},{8,7},{13,8},{10,9},{11,... | collective-permute-start | bytes 3145736 | tf_op jit(solution)/shard_map/ppermute | solution.py:231
  19.7 0.7 %copy-start.1 = (s32[170]{0:T(256)S(1)}, s32[170]{0:T(256)}, u32[]{:S(2)}) copy-start(s32[170]{0:T(256)} %sizes_ref.1) | copy-start | bytes 2044
  20.4 1.2 %copy-start = (bf16[512,1024]{1,0:T(8,128)(2,1)S(1)}, bf16[512,1024]{1,0:T(8,128)(2,1)}, u32[]{:S(2)}) copy-start(bf16[512,1024]{1,0:T(8,128)(2,1)} %raw_ref.1) | copy-start | bytes 3145732
  37.0 14.3 %collective-permute-start.3 = (f32[2,512]{1,0:T(2,128)S(1)}, f32[2,512]{1,0:T(2,128)S(1)}, u32[]{:S(2)}, u32[]{:S(2)}) collective-permute-start(f32[2,512]{1,0:T(2,128)S(1)} %get-tuple-element.27), channel_id=1, source_target_pairs={{4,0},{5,1},{6,2},{7,3},{8,4},{9,5},{10,6},{11,7},{12,8},{13,9},{1... | collective-permute-start | bytes 12296 | tf_op jit(solution)/shard_map/ppermute | solution.py:262
  45.2 8.2 %collective-permute-start.5 = (f32[2,512]{1,0:T(2,128)S(1)}, f32[2,512]{1,0:T(2,128)S(1)}, u32[]{:S(2)}, u32[]{:S(2)}) collective-permute-start(f32[2,512]{1,0:T(2,128)S(1)} %get-tuple-element.30), channel_id=1, source_target_pairs={{0,5},{1,2},{2,3},{3,4},{4,9},{5,6},{6,7},{7,8},{8,13},{9,10},{10,... | collective-permute-start | bytes 12296 | tf_op jit(solution)/shard_map/ppermute | solution.py:263
  47.2 4.9 %collective-permute-start.4 = (f32[2,512]{1,0:T(2,128)S(1)}, f32[2,512]{1,0:T(2,128)S(1)}, u32[]{:S(2)}, u32[]{:S(2)}) collective-permute-start(f32[2,512]{1,0:T(2,128)S(1)} %get-tuple-element.29), channel_id=1, source_target_pairs={{0,3},{1,0},{2,1},{3,2},{4,7},{5,4},{6,5},{7,6},{8,11},{9,8},{10,9... | collective-permute-start | bytes 12296 | tf_op jit(solution)/shard_map/ppermute | solution.py:264

commit v7 on v6

--- a/solution.py
+++ b/solution.py
@@ -160,14 +160,18 @@
             for i in lefts:
                 scores = score_block(slab[i][...], slab[j][span, :])
                 near = closeness_of(scores)
-                best[at[j], :, span] = jnp.maximum(best[at[j], :, span], fold_sublanes(scores, jnp.max))
-                count[at[j], :, span] = count[at[j], :, span] + fold_sublanes(near, jnp.sum)
+                high_cols, near_cols = fold_sublanes(scores, jnp.max), fold_sublanes(near, jnp.sum)
+                if i != lefts[0]:
+                    high_cols = jnp.maximum(best[at[j], :, span], high_cols)
+                    near_cols = count[at[j], :, span] + near_cols
+                best[at[j], :, span] = high_cols
+                count[at[j], :, span] = near_cols
                 high_part, near_part = fold_lanes(scores, jnp.maximum), fold_lanes(near, jnp.add)
                 high_rows[i] = high_part if start == 0 else jnp.maximum(high_rows[i], high_part)
                 near_rows[i] = near_part if start == 0 else near_rows[i] + near_part
         for i in lefts:
-            best[at[i]] = jnp.maximum(best[at[i]], fold_sublanes(high_rows[i].T, jnp.max))
-            count[at[i]] = count[at[i]] + fold_sublanes(near_rows[i].T, jnp.sum)
+            best[at[i]] = fold_sublanes(high_rows[i].T, jnp.max)
+            count[at[i]] = fold_sublanes(near_rows[i].T, jnp.sum)
 
     bits = jnp.max(mask_ref[...]).astype(jnp.int32)
     for flag, lefts, j in cases:

time: 54.4 us -> 54 us (level)
  starting transfers between devices: 31.9 us -> 31.3 us
where the time goes in v7:
time: 54 us; the launch traced here: 53.7 us
  starting transfers between devices  31.3 us (58%)
  waiting for transfers between devices  13.1 us (24%)
  Pallas kernels  6.13 us (11%)
  local copies, waits for them, and re-layouts  1.9 us (4%)
  between operations  0.76 us (1%)
  other arithmetic  0.6 us (1%)
    ppermute x1, starting transfers between devices, body(): down = lax.ppermute(embeddings, AXES, down_route)  11.5 us
    ppermute x1, waiting for transfers between devices, body(): below = lax.ppermute(embeddings, AXES, below_route)  10.7 us
    ppermute x1, starting transfers between devices, body(): from_below = lax.ppermute(for_below, AXES, inverse(below_route))  6.43 us
    ppermute x1, starting transfers between devices, body(): below = lax.ppermute(embeddings, AXES, below_route)  4.37 us
    pallas_call x1, Pallas kernels, diag_stats(): pl.pallas_call(functools.partial(diag_kernel, total), in_specs=[SMEM, SME...  4.05 us
    ppermute x1, starting transfers between devices, body(): from_up = lax.ppermute(for_up, AXES, inverse(up_route))  3.88 us
    ppermute x1, starting transfers between devices, body(): up = lax.ppermute(embeddings, AXES, up_route)  3.12 us
    pallas_call x3, Pallas kernels, pair_stats(): pl.pallas_call(functools.partial(pair_kernel, slots, given, cases, arrive...  2.07 us
  transfers between devices with their start and end apart: 6, of which 3 were waited for; matrix products, arithmetic and copies ran while one was open for 0% of the time, Pallas kernels for 11%

profile of v7, /device:TPU:1, one launch (start us, length us, event | category | flops | bytes accessed | tf_op | source)
XLA Modules:
  0.0 53.7 jit_solution(7116981917009669657)
XLA Ops:
  0.6 4.4 %collective-permute-start = (bf16[512,1024]{1,0:T(8,128)(2,1)}, bf16[512,1024]{1,0:T(8,128)(2,1)S(1)}, u32[]{:S(2)}, u32[]{:S(2)}) collective-permute-start(bf16[512,1024]{1,0:T(8,128)(2,1)} %raw_ref.1), channel_id=1, source_target_pairs={{0,4},{1,5},{2,6},{3,7},{4,8},{5,9},{6,10},{7,11},{8,12},{9,13},{1... | collective-permute-start | bytes 3145736 | tf_op jit(solution)/shard_map/ppermute | solution.py:233
  5.0 3.1 %collective-permute-start.1 = (bf16[512,1024]{1,0:T(8,128)(2,1)}, bf16[512,1024]{1,0:T(8,128)(2,1)S(1)}, u32[]{:S(2)}, u32[]{:S(2)}) collective-permute-start(bf16[512,1024]{1,0:T(8,128)(2,1)} %raw_ref.1), channel_id=1, source_target_pairs={{3,0},{0,1},{1,2},{2,3},{7,4},{4,5},{5,6},{6,7},{11,8},{8,9},{9,10... | collective-permute-start | bytes 3145736 | tf_op jit(solution)/shard_map/ppermute | solution.py:234
  8.1 11.5 %collective-permute-start.2 = (bf16[512,1024]{1,0:T(8,128)(2,1)}, bf16[512,1024]{1,0:T(8,128)(2,1)S(1)}, u32[]{:S(2)}, u32[]{:S(2)}) collective-permute-start(bf16[512,1024]{1,0:T(8,128)(2,1)} %raw_ref.1), channel_id=1, source_target_pairs={{5,0},{2,1},{3,2},{4,3},{9,4},{6,5},{7,6},{8,7},{13,8},{10,9},{11,... | collective-permute-start | bytes 3145736 | tf_op jit(solution)/shard_map/ppermute | solution.py:235
  19.7 0.0 copy-start.1
  19.7 0.7 %copy-done.1 = s32[170]{0:T(256)S(1)} copy-done((s32[170]{0:T(256)S(1)}, s32[170]{0:T(256)}, u32[]{:S(2)}) %copy-start.1) | copy-done | bytes 704
  20.4 0.0 copy-start
  20.4 1.2 %copy-done = bf16[512,1024]{1,0:T(8,128)(2,1)S(1)} copy-done((bf16[512,1024]{1,0:T(8,128)(2,1)S(1)}, bf16[512,1024]{1,0:T(8,128)(2,1)}, u32[]{:S(2)}) %copy-start) | copy-done | bytes 1048600
  21.6 4.1 %shard_map.41 = (f32[2,512]{1,0:T(2,128)S(1)}, f32[8,128]{1,0:T(8,128)S(1)}, bf16[512,1024]{1,0:T(8,128)(2,1)S(1)}) custom-call(s32[170]{0:T(256)S(1)} %copy-done.1, s32[1]{0:T(128)} %bitcast.place_ref, bf16[512,1024]{1,0:T(8,128)(2,1)S(1)} %copy-done), custom_call_target="tpu_custom_call" | custom-call | flops 536870912 | bytes 1048576 | tf_op jit(solution)/shard_map/pallas_call | solution.py:215
  25.6 10.7 %collective-permute-done.refs_1_ = bf16[512,1024]{1,0:T(8,128)(2,1)S(1)} collective-permute-done((bf16[512,1024]{1,0:T(8,128)(2,1)}, bf16[512,1024]{1,0:T(8,128)(2,1)S(1)}, u32[]{:S(2)}, u32[]{:S(2)}) %collective-permute-start) | collective-permute-done | bytes 1048608 | tf_op jit(solution)/shard_map/ppermute | solution.py:233
  36.3 0.2 shard_map.42
  36.5 0.0 collective-permute-done.1.refs_3_
  36.5 0.5 shard_map.43
  37.0 6.4 %collective-permute-start.3 = (f32[2,512]{1,0:T(2,128)S(1)}, f32[2,512]{1,0:T(2,128)S(1)}, u32[]{:S(2)}, u32[]{:S(2)}) collective-permute-start(f32[2,512]{1,0:T(2,128)S(1)} %get-tuple-element.27), channel_id=1, source_target_pairs={{4,0},{5,1},{6,2},{7,3},{8,4},{9,5},{10,6},{11,7},{12,8},{13,9},{1... | collective-permute-start | bytes 12296 | tf_op jit(solution)/shard_map/ppermute | solution.py:266
  43.5 0.0 collective-permute-done.2.refs_2_
  43.5 1.4 %shard_map.44 = (f32[2,512]{1,0:T(2,128)S(1)}, f32[2,512]{1,0:T(2,128)S(1)}, f32[2,512]{1,0:T(2,128)S(1)}) custom-call(f32[8,128]{1,0:T(8,128)S(1)} %get-tuple-element.17.mask_ref, f32[2,512]{1,0:T(2,128)S(1)} %get-tuple-element.23.refs_0_, f32[2,512]{1,0:T(2,128)S(1)} %get-tuple-element.24.refs_1_, bf16[512,1024]{1,0:T(8,128)(2,1)S(1)} %collective-permute-done.2.refs_2_, ...), custom_call_target="tpu_custom_call" | custom-call | flops 536870912 | bytes 3145728 | tf_op jit(solution)/shard_map/pallas_call | solution.py:201
  44.9 1.9 %collective-permute-start.5 = (f32[2,512]{1,0:T(2,128)S(1)}, f32[2,512]{1,0:T(2,128)S(1)}, u32[]{:S(2)}, u32[]{:S(2)}) collective-permute-start(f32[2,512]{1,0:T(2,128)S(1)} %get-tuple-element.30), channel_id=1, source_target_pairs={{0,5},{1,2},{2,3},{3,4},{4,9},{5,6},{6,7},{7,8},{8,13},{9,10},{10,... | collective-permute-start | bytes 12296 | tf_op jit(solution)/shard_map/ppermute | solution.py:267
  46.8 3.9 %collective-permute-start.4 = (f32[2,512]{1,0:T(2,128)S(1)}, f32[2,512]{1,0:T(2,128)S(1)}, u32[]{:S(2)}, u32[]{:S(2)}) collective-permute-start(f32[2,512]{1,0:T(2,128)S(1)} %get-tuple-element.29), channel_id=1, source_target_pairs={{0,3},{1,0},{2,1},{3,2},{4,7},{5,4},{6,5},{7,6},{8,11},{9,8},{10,9... | collective-permute-start | bytes 12296 | tf_op jit(solution)/shard_map/ppermute | solution.py:268
  50.7 0.0 collective-permute-done.3
  50.7 0.7 %collective-permute-done.4 = f32[2,512]{1,0:T(2,128)S(1)} collective-permute-done((f32[2,512]{1,0:T(2,128)S(1)}, f32[2,512]{1,0:T(2,128)S(1)}, u32[]{:S(2)}, u32[]{:S(2)}) %collective-permute-start.4) | collective-permute-done | bytes 4128 | tf_op jit(solution)/shard_map/ppermute | solution.py:268
  51.5 1.7 %collective-permute-done.5 = f32[2,512]{1,0:T(2,128)S(1)} collective-permute-done((f32[2,512]{1,0:T(2,128)S(1)}, f32[2,512]{1,0:T(2,128)S(1)}, u32[]{:S(2)}, u32[]{:S(2)}) %collective-permute-start.5) | collective-permute-done | bytes 4128 | tf_op jit(solution)/shard_map/ppermute | solution.py:267
  53.2 0.6 %add_add_fusion = (f32[512]{0:T(512)}, f32[512]{0:T(512)}) fusion(f32[512]{0:T(512)S(1)} %bitcast.9, f32[512]{0:T(512)S(1)} %bitcast.7, f32[512]{0:T(512)S(1)} %bitcast.11, f32[512]{0:T(512)S(1)} %bitcast.10, f32[512]{0:T(512)S(1)} %bitcast.8, f32[512]{0:T(512)S(1)} %bitcast.12), kind=kLoop, calls=%fused_computation.4 | loop fusion | flops 2048 | bytes 16384 | tf_op jit(solution)/shard_map/add | solution.py:276
  (3 shorter events, 0.0 us)
Async XLA Ops:
  0.6 35.7 %collective-permute-start = (bf16[512,1024]{1,0:T(8,128)(2,1)}, bf16[512,1024]{1,0:T(8,128)(2,1)S(1)}, u32[]{:S(2)}, u32[]{:S(2)}) collective-permute-start(bf16[512,1024]{1,0:T(8,128)(2,1)} %raw_ref.1), channel_id=1, source_target_pairs={{0,4},{1,5},{2,6},{3,7},{4,8},{5,9},{6,10},{7,11},{8,12},{9,13},{1... | collective-permute-start | bytes 3145736 | tf_op jit(solution)/shard_map/ppermute | solution.py:233
  5.0 31.5 %collective-permute-start.1 = (bf16[512,1024]{1,0:T(8,128)(2,1)}, bf16[512,1024]{1,0:T(8,128)(2,1)S(1)}, u32[]{:S(2)}, u32[]{:S(2)}) collective-permute-start(bf16[512,1024]{1,0:T(8,128)(2,1)} %raw_ref.1), channel_id=1, source_target_pairs={{3,0},{0,1},{1,2},{2,3},{7,4},{4,5},{5,6},{6,7},{11,8},{8,9},{9,10... | collective-permute-start | bytes 3145736 | tf_op jit(solution)/shard_map/ppermute | solution.py:234
  8.1 35.3 %collective-permute-start.2 = (bf16[512,1024]{1,0:T(8,128)(2,1)}, bf16[512,1024]{1,0:T(8,128)(2,1)S(1)}, u32[]{:S(2)}, u32[]{:S(2)}) collective-permute-start(bf16[512,1024]{1,0:T(8,128)(2,1)} %raw_ref.1), channel_id=1, source_target_pairs={{5,0},{2,1},{3,2},{4,3},{9,4},{6,5},{7,6},{8,7},{13,8},{10,9},{11,... | collective-permute-start | bytes 3145736 | tf_op jit(solution)/shard_map/ppermute | solution.py:235
  19.7 0.7 %copy-start.1 = (s32[170]{0:T(256)S(1)}, s32[170]{0:T(256)}, u32[]{:S(2)}) copy-start(s32[170]{0:T(256)} %sizes_ref.1) | copy-start | bytes 2044
  20.4 1.2 %copy-start = (bf16[512,1024]{1,0:T(8,128)(2,1)S(1)}, bf16[512,1024]{1,0:T(8,128)(2,1)}, u32[]{:S(2)}) copy-start(bf16[512,1024]{1,0:T(8,128)(2,1)} %raw_ref.1) | copy-start | bytes 3145732
  37.0 13.7 %collective-permute-start.3 = (f32[2,512]{1,0:T(2,128)S(1)}, f32[2,512]{1,0:T(2,128)S(1)}, u32[]{:S(2)}, u32[]{:S(2)}) collective-permute-start(f32[2,512]{1,0:T(2,128)S(1)} %get-tuple-element.27), channel_id=1, source_target_pairs={{4,0},{5,1},{6,2},{7,3},{8,4},{9,5},{10,6},{11,7},{12,8},{13,9},{1... | collective-permute-start | bytes 12296 | tf_op jit(solution)/shard_map/ppermute | solution.py:266
  44.9 8.2 %collective-permute-start.5 = (f32[2,512]{1,0:T(2,128)S(1)}, f32[2,512]{1,0:T(2,128)S(1)}, u32[]{:S(2)}, u32[]{:S(2)}) collective-permute-start(f32[2,512]{1,0:T(2,128)S(1)} %get-tuple-element.30), channel_id=1, source_target_pairs={{0,5},{1,2},{2,3},{3,4},{4,9},{5,6},{6,7},{7,8},{8,13},{9,10},{10,... | collective-permute-start | bytes 12296 | tf_op jit(solution)/shard_map/ppermute | solution.py:267
  46.8 4.6 %collective-permute-start.4 = (f32[2,512]{1,0:T(2,128)S(1)}, f32[2,512]{1,0:T(2,128)S(1)}, u32[]{:S(2)}, u32[]{:S(2)}) collective-permute-start(f32[2,512]{1,0:T(2,128)S(1)} %get-tuple-element.29), channel_id=1, source_target_pairs={{0,3},{1,0},{2,1},{3,2},{4,7},{5,4},{6,5},{7,6},{8,11},{9,8},{10,9... | collective-permute-start | bytes 12296 | tf_op jit(solution)/shard_map/ppermute | solution.py:268
